TPU v7x, 256 devices: a whole 4x4x8 slice. The times are simulated.
256 devices in a mesh: grp: 2 (over x_lo), gx: 16 (over z, core), gy: 8 (over y, x_hi).
Axes of the slice: x: 4 (x_hi: 2, x_lo: 2; x = x_hi * 2 + x_lo), y: 4, z: 8, core: 2. Of those that a mesh axis runs over, the one named last changes fastest.
Arguments:
- base_flow: float32 [128, 128, 256], P('gx', 'gy', 'grp'), may hold values from -4 to 4
- fields: float32 [16, 128, 128, 256], P('grp', 'gx', 'gy'), may hold values from -80 to 80, as said below
- wall_mask: int32 [128, 256], P('gy'), may hold values 0 or 1
- conduct_flag: int32 [128, 256], P('gy'), may hold values 0 or 1
Outputs:
- base_out: float32 [128, 128, 256], P('gx', 'gy', 'grp')
- ortho_fields: float32 [16, 128, 128, 256], P('grp', 'gx', 'gy')
- growth: float32 [16], replicated
Inputs may be any that keep to these rules, and one draw needn't show every extreme that they name: real-valued perturbation fields.
All inputs are finite; a program needn't handle non-finite values. No bound on the sum of `wall_mask` or of `conduct_flag` on one device may be relied on, other than what follows from the above.
Results may differ from a plain program's by a relative error of at most 0.00011.
Values sent between devices are 32-bit elements; how exact they have to be, the bound alone decides.
A program may use at most 64 MiB of HBM per device.

v0:
```python
import jax
import jax.numpy as jnp
from jax import lax
from jax.sharding import PartitionSpec as P

STEPS = 2


step_dt = 0.15
drive = 0.5


def with_halo(block, sides, width, periodic):
    for axis, dim in sides:
        count = lax.axis_size(axis)
        forward = [(i, i + 1) for i in range(count - 1)]
        if periodic:
            forward.append((count - 1, 0))
        backward = [(target, source) for source, target in forward]
        low = lax.ppermute(
            lax.slice_in_dim(block, block.shape[dim] - width, None, axis=dim), axis, forward
        )
        high = lax.ppermute(lax.slice_in_dim(block, 0, width, axis=dim), axis, backward)
        block = jnp.concatenate([low, block, high], axis=dim)
    return block


def surround(stack):
    wider = with_halo(stack, (("gx", 1),), 1, True)
    return with_halo(wider, (("gy", 2),), 1, False)


def derivs(padded):
    centre = padded[:, 1:-1, 1:-1, 1:-1]
    beside = padded[:, 2:, 1:-1, 1:-1] + padded[:, :-2, 1:-1, 1:-1]
    beside = beside + padded[:, 1:-1, 2:, 1:-1] + padded[:, 1:-1, :-2, 1:-1]
    beside = beside + padded[:, 1:-1, 1:-1, 2:] + padded[:, 1:-1, 1:-1, :-2]
    slope = (padded[:, 2:, 1:-1, 1:-1] - padded[:, :-2, 1:-1, 1:-1]) * 0.5
    return (centre, beside - 6.0 * centre, slope)


def body(base_flow, fields, wall_mask, conduct_flag):
    half = base_flow.shape[2]
    group = lax.axis_index("grp")
    wall_full = wall_mask.astype(jnp.float32)
    damp_full = 0.25 * (1.0 + 3.0 * conduct_flag.astype(jnp.float32))
    base = base_flow
    working = fields
    for step in range(STEPS):
        whole = lax.all_gather(base, "grp", axis=2, tiled=True)
        padded = surround(jnp.concatenate([whole[None], working], 0))
        padded = jnp.pad(padded, ((0, 0), (0, 0), (0, 0), (1, 1)))
        centre, lap_all, dx_all = derivs(padded)
        speed = centre[0]
        dx_speed = dx_all[0]
        inner = centre[1:]
        working = wall_full * (
            inner
            + step_dt * (lap_all[1:] - speed * dx_all[1:] - inner * dx_speed - damp_full * inner)
        )
        stepped = wall_full * (
            speed + step_dt * (lap_all[0] - speed * dx_speed - damp_full * speed + drive)
        )
        base = lax.dynamic_slice_in_dim(stepped, group * half, half, 2)
    total_cells = (
        base.shape[0]
        * lax.axis_size("gx")
        * base.shape[1]
        * lax.axis_size("gy")
        * half
        * lax.axis_size("grp")
    )
    spanwise = lax.all_to_all(working, "grp", split_axis=3, concat_axis=0, tiled=True)
    every = spanwise.shape[0]
    flat = spanwise.reshape(every, -1)
    partial_gram = jnp.dot(flat, flat.T, precision=lax.Precision.HIGHEST)
    gram = lax.psum(partial_gram, ("grp", "gx", "gy")) / float(total_cells)
    lower = jnp.linalg.cholesky(gram)
    inverse = jax.scipy.linalg.solve_triangular(
        lower, jnp.eye(every, dtype=jnp.float32), lower=True
    )
    renormed = jnp.dot(inverse, flat, precision=lax.Precision.HIGHEST).reshape(spanwise.shape)
    ortho = lax.all_to_all(renormed, "grp", split_axis=0, concat_axis=3, tiled=True)
    growth = jnp.log(jnp.diagonal(lower))
    return (base, ortho, growth)


def solution(mesh):
    in_specs = (P("gx", "gy", "grp"), P("grp", "gx", "gy", None), P("gy", None), P("gy", None))
    out_specs = (P("gx", "gy", "grp"), P("grp", "gx", "gy", None), P())
    return jax.shard_map(body, mesh=mesh, in_specs=in_specs, out_specs=out_specs, check_vma=False)
```

profile of v0, /device:TPU:1, one launch (start us, length us, event | category | flops | bytes accessed | tf_op | source)
XLA Modules:
  0.0 223.6 jit_solution(12748432022173113342)
XLA Ops:
  0.6 0.0 copy-start
  0.7 4.8 %all_gather.6 = f32[8,16,256]{2,1,0:T(8,128)S(1)} all-gather(f32[8,16,128]{2,1,0:T(8,128)} %param.4), channel_id=1, replica_groups=mesh['grp'=2,'gx'=16,'gy'=8] {'grp'}, dimensions={2}, use_global_device_ids=true | all-gather | bytes 196608 | tf_op jit(solution)/shard_map/all_gather | solution.py:50
  5.4 1.0 fusion.26
  6.4 3.8 %collective-permute-start = (f32[9,1,16,256]{3,2,1,0:T(8,128)S(1)}, f32[9,1,16,256]{3,2,1,0:T(8,128)S(1)}, u32[]{:S(2)}, u32[]{:S(2)}) collective-permute-start(f32[9,1,16,256]{3,2,1,0:T(8,128)S(1)} %get-tuple-element.15), channel_id=1, source_target_pairs={{8,0},{16,8},{24,16},{32,24},{40,32},{48,40},{56,48},{64,56},{72,6... | collective-permute-start | bytes 442376 | tf_op jit(solution)/shard_map/ppermute | solution.py:23
  10.2 0.0 collective-permute-start.1
  10.2 0.0 copy-done.7
  10.2 0.0 copy-start.2
  10.3 2.5 %collective-permute-done = f32[9,1,16,256]{3,2,1,0:T(8,128)S(1)} collective-permute-done((f32[9,1,16,256]{3,2,1,0:T(8,128)S(1)}, f32[9,1,16,256]{3,2,1,0:T(8,128)S(1)}, u32[]{:S(2)}, u32[]{:S(2)}) %collective-permute-start) | collective-permute-done | bytes 147488 | tf_op jit(solution)/shard_map/ppermute | solution.py:23
  12.8 0.7 collective-permute-done.1
  13.5 0.2 subtract_multiply_fusion.1
  13.7 0.1 pad_maximum_fusion.30
  13.8 1.3 collective-permute-start.2
  15.1 5.5 %collective-permute-start.3 = (f32[9,10,1,256]{3,2,1,0:T(1,128)S(1)}, f32[9,10,1,256]{3,2,1,0:T(1,128)S(1)}, u32[]{:S(2)}, u32[]{:S(2)}) collective-permute-start(f32[9,10,1,256]{3,2,1,0:T(1,128)S(1)} %get-tuple-element.10), channel_id=1, source_target_pairs={{0,1},{1,2},{2,3},{3,4},{4,5},{5,6},{6,7},{8,9},{9,10},{10,11},{11... | collective-permute-start | bytes 276488 | tf_op jit(solution)/shard_map/ppermute | solution.py:20
  20.6 0.0 collective-permute-done.2
  20.6 1.5 collective-permute-done.3
  22.2 3.0 %select_maximum_fusion.5 = f32[9,10,18,258]{3,2,1,0:T(8,128)S(1)} fusion(f32[9,10,1,256]{3,2,1,0:T(1,128)S(1)} %collective-permute-done.2, f32[9,10,1,256]{3,2,1,0:T(1,128)S(1)} %collective-permute-done.3, f32[9,1,16,256]{3,2,1,0:T(8,128)S(1)} %collective-permute-done, f32[9,1,16,256]{3,2,1,0:T(8,128)S(1)} %collective-permute-done.1, ...), kind=kLoop, calls=%fused_computation.8 | loop fusion | flops 5851440 | bytes 3330720 | tf_op jit(solution)/shard_map/concatenate | solution.py:24
  25.2 1.3 fusion.4
  26.5 0.0 copy-done.4
  26.6 3.8 %all_gather.7 = f32[8,16,256]{2,1,0:T(8,128)S(1)} all-gather(f32[8,16,128]{2,1,0:T(8,128)S(1)} %fusion.36), channel_id=1, replica_groups=mesh['grp'=2,'gx'=16,'gy'=8] {'grp'}, dimensions={2}, use_global_device_ids=true | all-gather | bytes 196608 | tf_op jit(solution)/shard_map/all_gather | solution.py:50
  30.4 0.4 fusion.20
  30.8 7.2 %collective-permute-start.4 = (f32[9,1,16,256]{3,2,1,0:T(8,128)S(1)}, f32[9,1,16,256]{3,2,1,0:T(8,128)S(1)}, u32[]{:S(2)}, u32[]{:S(2)}) collective-permute-start(f32[9,1,16,256]{3,2,1,0:T(8,128)S(1)} %get-tuple-element.13), channel_id=1, source_target_pairs={{8,0},{16,8},{24,16},{32,24},{40,32},{48,40},{56,48},{64,56},{72,6... | collective-permute-start | bytes 442376 | tf_op jit(solution)/shard_map/ppermute | solution.py:23
  38.1 0.0 collective-permute-start.5
  38.1 1.0 collective-permute-done.4
  39.1 1.1 collective-permute-done.5
  40.2 0.1 pad_maximum_fusion.26
  40.3 1.3 collective-permute-start.6
  41.6 6.2 %collective-permute-start.7 = (f32[9,10,1,256]{3,2,1,0:T(1,128)S(1)}, f32[9,10,1,256]{3,2,1,0:T(1,128)S(1)}, u32[]{:S(2)}, u32[]{:S(2)}) collective-permute-start(f32[9,10,1,256]{3,2,1,0:T(1,128)S(1)} %get-tuple-element.8), channel_id=1, source_target_pairs={{0,1},{1,2},{2,3},{3,4},{4,5},{5,6},{6,7},{8,9},{9,10},{10,11},{11... | collective-permute-start | bytes 276488 | tf_op jit(solution)/shard_map/ppermute | solution.py:20
  47.8 0.2 subtract_multiply_fusion
  48.0 0.0 collective-permute-done.6
  48.0 1.3 collective-permute-done.7
  49.4 3.0 %select_maximum_fusion = f32[9,10,18,258]{3,2,1,0:T(8,128)S(1)} fusion(f32[9,10,1,256]{3,2,1,0:T(1,128)S(1)} %collective-permute-done.6, f32[9,10,1,256]{3,2,1,0:T(1,128)S(1)} %collective-permute-done.7, f32[9,1,16,256]{3,2,1,0:T(8,128)S(1)} %collective-permute-done.4, f32[9,1,16,256]{3,2,1,0:T(8,128)S(1)} %collective-permute-done.5, ...), kind=kLoop, calls=%fused_computation.3 | loop fusion | flops 5851440 | bytes 3330720 | tf_op jit(solution)/shard_map/concatenate | solution.py:24
  52.4 0.0 copy-start.3
  52.4 1.3 fusion.2
  53.7 0.4 fusion.14
  54.2 7.5 %copy.39 = f32[8,8,16,256]{2,1,0,3:T(8,128)} copy(f32[8,8,16,256]{3,2,1,0:T(8,128)S(1)} %fusion.14) | data formatting | bytes 2097152 | tf_op jit(solution)/shard_map/mul | solution.py:57
  61.6 6.0 %reshape.38 = f32[2,1,131072]{2,1,0:T(1,128)} reshape(f32[256,8,8,16]{3,2,1,0:T(8,128)} %bitcast.51) | data formatting | bytes 2097152
  67.6 3.8 %all-to-all-start = ((f32[2,1,131072]{2,1,0:T(1,128)}), f32[2,1,131072]{2,1,0:T(1,128)S(1)}, u32[]{:S(2)}, u32[]{:S(2)}) async-start(f32[2,1,131072]{2,1,0:T(1,128)} %reshape.38), calls=%async_computation | async-start | bytes 2097152 | tf_op jit(solution)/shard_map/all_to_all | solution.py:73
  71.4 8.9 %all-to-all-done = f32[2,1,131072]{2,1,0:T(1,128)S(1)} async-done(((f32[2,1,131072]{2,1,0:T(1,128)}), f32[2,1,131072]{2,1,0:T(1,128)S(1)}, u32[]{:S(2)}, u32[]{:S(2)}) %all-to-all-start) | async-done | bytes 1048608 | tf_op jit(solution)/shard_map/all_to_all | solution.py:73
  80.3 1.0 copy-done.1
  81.3 0.5 broadcast.161
  81.8 4.9 %reduce.6 = f32[2,131072]{1,0:T(2,128)S(1)} reduce(f32[2,1,131072]{2,1,0:T(1,128)} %copy-done.1, f32[]{:T(128)} %broadcast.161), dimensions={1}, to_apply=%all_to_all.24.reduce_sub_computation | reduce | bytes 2097156 | tf_op jit(solution)/shard_map/all_to_all | solution.py:73
  86.7 6.0 %reshape.39 = f32[256,8,8,16]{3,2,1,0:T(8,128)} reshape(f32[2,131072]{1,0:T(2,128)S(1)} %reduce.6) | data formatting | bytes 2097152
  92.7 7.4 %copy.40 = f32[8,8,16,2,128]{4,2,1,0,3:T(8,128)} copy(f32[8,8,16,2,128]{2,1,0,4,3:T(8,128)} %bitcast.52) | data formatting | bytes 2097152 | tf_op jit(solution)/shard_map/all_to_all | solution.py:73
  100.1 1.4 reshape.30
  101.5 2.1 fusion.41
  103.6 87.3 %psum.7 = f32[16,16]{0,1:T(8,128)S(1)} all-reduce(f32[16,16]{0,1:T(8,128)} %fusion.41), channel_id=1, replica_groups=mesh['grp'=2,'gx'=16,'gy'=8] {'grp','gx','gy'}, use_global_device_ids=true, to_apply=%region_0.1 | all-reduce | flops 256 | bytes 2048 | tf_op jit(solution)/shard_map/psum | solution.py:77
  190.9 0.6 broadcast_multiply_fusion
  191.5 1.4 copy.42
  192.9 1.3 fusion.38
  194.2 2.1 cholesky.17
  196.4 0.6 copy-done.6
  197.0 0.6 compare_reduce_fusion
  197.6 1.9 select_bitcast_fusion
  199.6 2.5 %custom-call.7 = f32[1,16,16]{1,2,0:T(8,128)} custom-call(f32[1,16,16]{2,1,0:T(8,128)} %get-tuple-element.6), custom_call_target="InvertDiagBlocksLowerTriangular" | custom-call | tf_op jit(solution)/shard_map/jit(_solve_triangular)/triangular_solve | solution.py:79
  202.1 0.9 convolution_bitcast_fusion
  203.0 0.2 copy.49
  203.2 1.5 fusion.21
  204.7 1.3 copy.44
  206.0 3.6 %all-to-all-start.1 = ((f32[16,8,16,128]{3,2,1,0:T(8,128)}), f32[16,8,16,128]{3,2,1,0:T(8,128)S(1)}, u32[]{:S(2)}, u32[]{:S(2)}) async-start(f32[16,8,16,128]{3,2,1,0:T(8,128)} %copy.44), calls=%async_computation.1 | async-start | bytes 2097152 | tf_op jit(solution)/shard_map/all_to_all | solution.py:83
  209.6 1.4 fusion.31
  211.0 0.7 gather_fusion
  211.6 0.5 log.3
  212.2 10.4 %all-to-all-done.1 = f32[16,8,16,128]{3,2,1,0:T(8,128)S(1)} async-done(((f32[16,8,16,128]{3,2,1,0:T(8,128)}), f32[16,8,16,128]{3,2,1,0:T(8,128)S(1)}, u32[]{:S(2)}, u32[]{:S(2)}) %all-to-all-start.1) | async-done | bytes 1048608 | tf_op jit(solution)/shard_map/all_to_all | solution.py:83
  222.5 1.1 copy.53
  (25 shorter events, 0.2 us)
Async XLA Ops:
  0.6 12.8 %copy-start = (f32[8,8,16,256]{3,2,1,0:T(8,128)S(1)}, f32[8,8,16,256]{3,2,1,0:T(8,128)}, u32[]{:S(2)}) copy-start(f32[8,8,16,256]{3,2,1,0:T(8,128)} %param.5) | copy-start | bytes 3145732
  0.6 9.6 %copy-start.7 = (s32[16,256]{1,0:T(8,128)S(1)}, s32[16,256]{1,0:T(8,128)}, u32[]{:S(2)}) copy-start(s32[16,256]{1,0:T(8,128)} %param.6) | copy-start | bytes 49156
  0.7 9.6 %copy-start.8 = (s32[16,256]{1,0:T(8,128)S(1)}, s32[16,256]{1,0:T(8,128)}, u32[]{:S(2)}) copy-start(s32[16,256]{1,0:T(8,128)} %param.7) | copy-start | bytes 49156
  6.4 6.4 %collective-permute-start = (f32[9,1,16,256]{3,2,1,0:T(8,128)S(1)}, f32[9,1,16,256]{3,2,1,0:T(8,128)S(1)}, u32[]{:S(2)}, u32[]{:S(2)}) collective-permute-start(f32[9,1,16,256]{3,2,1,0:T(8,128)S(1)} %get-tuple-element.15), channel_id=1, source_target_pairs={{8,0},{16,8},{24,16},{32,24},{40,32},{48,40},{56,48},{64,56},{72,6... | collective-permute-start | bytes 442376 | tf_op jit(solution)/shard_map/ppermute | solution.py:23
  10.2 3.3 %collective-permute-start.1 = (f32[9,1,16,256]{3,2,1,0:T(8,128)S(1)}, f32[9,1,16,256]{3,2,1,0:T(8,128)S(1)}, u32[]{:S(2)}, u32[]{:S(2)}) collective-permute-start(f32[9,1,16,256]{3,2,1,0:T(8,128)S(1)} %get-tuple-element.14), channel_id=1, source_target_pairs={{0,8},{8,16},{16,24},{24,32},{32,40},{40,48},{48,56},{56,64},{64,7... | collective-permute-start | bytes 442376 | tf_op jit(solution)/shard_map/ppermute | solution.py:20
  10.2 20.2 %copy-start.2 = (f32[16,256]{1,0:T(8,128)}, f32[16,256]{1,0:T(8,128)S(1)}, u32[]{:S(2)}) copy-start(f32[16,256]{1,0:T(8,128)S(1)} %add_multiply_fusion) | copy-start | bytes 49156
  10.3 16.3 %copy-start.4 = (f32[16,128]{1,0:T(8,128)}, f32[16,128]{1,0:T(8,128)S(1)}, u32[]{:S(2)}) copy-start(f32[16,128]{1,0:T(8,128)S(1)} %constant_dynamic-slice_fusion) | copy-start | bytes 24580
  10.3 16.2 %copy-start.5 = (f32[16,128]{1,0:T(8,128)}, f32[16,128]{1,0:T(8,128)S(1)}, u32[]{:S(2)}) copy-start(f32[16,128]{1,0:T(8,128)S(1)} %constant_dynamic-slice_fusion.1) | copy-start | bytes 24580
  13.8 6.8 %collective-permute-start.2 = (f32[9,10,1,256]{3,2,1,0:T(1,128)S(1)}, f32[9,10,1,256]{3,2,1,0:T(1,128)S(1)}, u32[]{:S(2)}, u32[]{:S(2)}) collective-permute-start(f32[9,10,1,256]{3,2,1,0:T(1,128)S(1)} %get-tuple-element.11), channel_id=1, source_target_pairs={{1,0},{2,1},{3,2},{4,3},{5,4},{6,5},{7,6},{9,8},{10,9},{11,10},{12... | collective-permute-start | bytes 276488 | tf_op jit(solution)/shard_map/ppermute | solution.py:23
  15.1 7.1 %collective-permute-start.3 = (f32[9,10,1,256]{3,2,1,0:T(1,128)S(1)}, f32[9,10,1,256]{3,2,1,0:T(1,128)S(1)}, u32[]{:S(2)}, u32[]{:S(2)}) collective-permute-start(f32[9,10,1,256]{3,2,1,0:T(1,128)S(1)} %get-tuple-element.10), channel_id=1, source_target_pairs={{0,1},{1,2},{2,3},{3,4},{4,5},{5,6},{6,7},{8,9},{9,10},{10,11},{11... | collective-permute-start | bytes 276488 | tf_op jit(solution)/shard_map/ppermute | solution.py:20
  30.8 8.2 %collective-permute-start.4 = (f32[9,1,16,256]{3,2,1,0:T(8,128)S(1)}, f32[9,1,16,256]{3,2,1,0:T(8,128)S(1)}, u32[]{:S(2)}, u32[]{:S(2)}) collective-permute-start(f32[9,1,16,256]{3,2,1,0:T(8,128)S(1)} %get-tuple-element.13), channel_id=1, source_target_pairs={{8,0},{16,8},{24,16},{32,24},{40,32},{48,40},{56,48},{64,56},{72,6... | collective-permute-start | bytes 442376 | tf_op jit(solution)/shard_map/ppermute | solution.py:23
  38.1 2.1 collective-permute-start.5
  40.3 7.7 %collective-permute-start.6 = (f32[9,10,1,256]{3,2,1,0:T(1,128)S(1)}, f32[9,10,1,256]{3,2,1,0:T(1,128)S(1)}, u32[]{:S(2)}, u32[]{:S(2)}) collective-permute-start(f32[9,10,1,256]{3,2,1,0:T(1,128)S(1)} %get-tuple-element.9), channel_id=1, source_target_pairs={{1,0},{2,1},{3,2},{4,3},{5,4},{6,5},{7,6},{9,8},{10,9},{11,10},{12... | collective-permute-start | bytes 276488 | tf_op jit(solution)/shard_map/ppermute | solution.py:23
  41.6 7.8 %collective-permute-start.7 = (f32[9,10,1,256]{3,2,1,0:T(1,128)S(1)}, f32[9,10,1,256]{3,2,1,0:T(1,128)S(1)}, u32[]{:S(2)}, u32[]{:S(2)}) collective-permute-start(f32[9,10,1,256]{3,2,1,0:T(1,128)S(1)} %get-tuple-element.8), channel_id=1, source_target_pairs={{0,1},{1,2},{2,3},{3,4},{4,5},{5,6},{6,7},{8,9},{9,10},{10,11},{11... | collective-permute-start | bytes 276488 | tf_op jit(solution)/shard_map/ppermute | solution.py:20
  52.4 1.3 copy-start.3
  67.6 12.6 %all-to-all-start = ((f32[2,1,131072]{2,1,0:T(1,128)}), f32[2,1,131072]{2,1,0:T(1,128)S(1)}, u32[]{:S(2)}, u32[]{:S(2)}) async-start(f32[2,1,131072]{2,1,0:T(1,128)} %reshape.38), calls=%async_computation | async-start | bytes 2097152 | tf_op jit(solution)/shard_map/all_to_all | solution.py:73
  80.3 1.0 copy-start.1
  196.4 0.6 copy-start.6
  206.0 16.6 %all-to-all-start.1 = ((f32[16,8,16,128]{3,2,1,0:T(8,128)}), f32[16,8,16,128]{3,2,1,0:T(8,128)S(1)}, u32[]{:S(2)}, u32[]{:S(2)}) async-start(f32[16,8,16,128]{3,2,1,0:T(8,128)} %copy.44), calls=%async_computation.1 | async-start | bytes 2097152 | tf_op jit(solution)/shard_map/all_to_all | solution.py:83
where the time goes:
time: 225 us; the launch traced here: 224 us
  blocking collectives  95.9 us (43%)
  local copies, waits for them, and re-layouts  35.6 us (16%)
  starting transfers between devices  32.6 us (14%)
  waiting for transfers between devices  27.4 us (12%)
  other arithmetic  26.7 us (12%)
  matrix products  4.47 us (2%)
    psum x1, blocking collectives, body(): gram = lax.psum(partial_gram, ('grp', 'gx', 'gy')) / float(total_cells)  87.3 us
    unnamed x21, local copies, waits for them, and re-layouts  13.8 us
    ppermute x4, starting transfers between devices, with_halo(): lax.ppermute(lax.slice_in_dim(block, 0, width, axis=dim), axis, backward)  13.6 us
    ppermute x4, starting transfers between devices, with_halo(): lax.ppermute(lax.slice_in_dim(block, block.shape[dim] - width, None, axis...  11.7 us
    all_to_all x1, waiting for transfers between devices, body(): lax.all_to_all(renormed, 'grp', split_axis=0, concat_axis=3, tiled=True)  10.4 us
    all_to_all x1, waiting for transfers between devices, body(): lax.all_to_all(working, 'grp', split_axis=3, concat_axis=0, tiled=True)  8.86 us
    all_gather x2, blocking collectives, body(): whole = lax.all_gather(base, 'grp', axis=2, tiled=True)  8.55 us
    all_to_all x2, local copies, waits for them, and re-layouts, body(): lax.all_to_all(working, 'grp', split_axis=3, concat_axis=0, tiled=True)  7.89 us
  transfers between devices with their start and end apart: 10, of which 8 were waited for; matrix products, arithmetic and copies ran while one was open for 1% of the time, Pallas kernels for 0%

commit v1 on v0

v1 whole, which is shorter than its diff:
```python
import jax
import jax.numpy as jnp
from jax import lax
from jax.experimental import pallas as pl
from jax.experimental.pallas import tpu as pltpu
from jax.sharding import PartitionSpec as P

MESH = pl.DeviceIdType.MESH
F32 = jnp.float32
GX, GY = 16, 8
LX, LY, NF, NZ = 8, 16, 8, 256
HALF = NZ // 2
CELLS = 4194304.0
P_ORDER = (4, 3, 5, 2, 6, 1, 7, 0)
Z_ORDER = (8, 7, 9, 6, 10, 5, 11, 4, 12, 3, 13, 2, 14, 1, 15)


def when(cond, fn):
    if cond is None:
        fn()
    else:
        pl.when(cond)(fn)


def remote(src, dst, send, recv, device):
    return pltpu.make_async_remote_copy(
        src_ref=src,
        dst_ref=dst,
        send_sem=send,
        recv_sem=recv,
        device_id=device,
        device_id_type=MESH,
    )


def both(*conds):
    out = None
    for c in conds:
        if c is not None:
            out = c if out is None else jnp.logical_and(out, c)
    return out


def kernel(
    base_hbm, fields_hbm, wall_ref, cond_ref,
    base_out, ortho_hbm, growth_out,
    fi, v1, w, o, ue, u1, wc, tile, al, zl, gs,
    ld_sem, out_sem, h_send, h_recv, x_send, x_recv, p_send, p_recv, z_send, z_recv,
):
    g = lax.axis_index("grp")
    gx = lax.axis_index("gx")
    gy = lax.axis_index("gy")
    other = 1 - g
    partner = (other, gx, gy)
    has_low = gy > 0
    has_high = gy < GY - 1
    lanes = pl.ds(pl.multiple_of(g * HALF, HALF), HALF)

    loads = [
        pltpu.make_async_copy(
            fields_hbm.at[f], fi.at[pl.ds(2, LX), pl.ds(2, LY), f], ld_sem.at[f]
        )
        for f in range(NF)
    ]
    loads.append(
        pltpu.make_async_copy(base_hbm, ue.at[pl.ds(2, LX), pl.ds(8, LY), lanes], ld_sem.at[NF])
    )
    for c in loads:
        c.start()

    barrier = pltpu.get_barrier_semaphore()
    count = 0
    greet = []
    for dx in (-1, 0, 1):
        for dy in (-1, 0, 1):
            for side in (0, 1):
                if dx == 0 and dy == 0 and side == 0:
                    continue
                ok = None if dy == 0 else (has_low if dy < 0 else has_high)
                who = g if side == 0 else other
                greet.append((ok, (who, lax.rem(gx + dx + GX, GX), gy + dy)))
    for y in range(GY):
        far = jnp.abs(gy - y) >= 2
        greet.append((far, (1, gx, y)))
        greet.append((both(far, g == 1), (0, gx, y)))
    for off in range(2, GX - 1):
        greet.append((g == 1, (1, lax.rem(gx + off, GX), gy)))
    for ok, dev in greet:
        when(
            ok,
            lambda dev=dev: pl.semaphore_signal(
                barrier, inc=1, device_id=dev, device_id_type=MESH
            ),
        )
        count = count + (1 if ok is None else jnp.where(ok, 1, 0))

    wc[0, pl.ds(8, LY), :] = wall_ref[...].astype(F32)
    wc[1, pl.ds(8, LY), :] = 0.1 - 0.15 * (0.25 * (1.0 + 3.0 * cond_ref[...].astype(F32)))

    for ok, row, urow, wrow in ((gy == 0, 0, 6, 7), (gy == GY - 1, LY + 2, 24, 24)):

        def clear(row=row, urow=urow, wrow=wrow):
            for x in range(LX + 4):
                fi[x, pl.ds(row, 2)] = jnp.zeros((2, NF, NZ), F32)
                ue[x, pl.ds(urow, 2), :] = jnp.zeros((2, NZ), F32)
            for i in range(2):
                wc[i, pl.ds(wrow, 1), :] = jnp.zeros((1, NZ), F32)

        pl.when(ok)(clear)

    for c in loads:
        c.wait()
    pl.semaphore_wait(barrier, count)

    halos = []

    def halo(dx, dy, src, dst, who=None):
        to = None if dy == 0 else (has_low if dy < 0 else has_high)
        frm = None if dy == 0 else (has_high if dy < 0 else has_low)
        i = len(halos)
        dev = (g if who is None else who, lax.rem(gx + dx + GX, GX), gy + dy)
        halos.append((to, frm, remote(src, dst, h_send.at[i], h_recv.at[i], dev)))

    xs, ys = pl.ds(2, LX), pl.ds(2, LY)
    yu = pl.ds(8, LY)
    for dy, src, dst in ((-1, 2, LY + 2), (1, LY, 0)):
        halo(0, dy, fi.at[xs, pl.ds(src, 2)], fi.at[xs, pl.ds(dst, 2)])
    for dx, src, dst in ((-1, 2, LX + 2), (1, LX, 0)):
        halo(dx, 0, fi.at[pl.ds(src, 2), ys], fi.at[pl.ds(dst, 2), ys])
    src = ue.at[xs, yu, lanes]
    halo(0, 0, src, src, other)
    for who in (None, other):
        for dy, s, d in ((-1, 8, 24), (1, 22, 6)):
            halo(0, dy, ue.at[xs, pl.ds(s, 2), lanes], ue.at[xs, pl.ds(d, 2), lanes], who)
        for dx, s, d in ((-1, 2, LX + 2), (1, LX, 0)):
            halo(dx, 0, ue.at[pl.ds(s, 2), yu, lanes], ue.at[pl.ds(d, 2), yu, lanes], who)
        for dx, sx, tx in ((-1, 2, LX + 2), (1, LX + 1, 1)):
            for dy, sy, ty in ((-1, 8, 24), (1, 23, 7)):
                halo(
                    dx, dy,
                    ue.at[sx, pl.ds(sy, 1), lanes], ue.at[tx, pl.ds(ty, 1), lanes], who,
                )
    for dx, sx, tx in ((-1, 2, LX + 2), (1, LX + 1, 1)):
        for dy, sy, ty in ((-1, 2, LY + 2), (1, LY + 1, 1)):
            halo(dx, dy, fi.at[sx, sy], fi.at[tx, ty])
    for dy, s, d in ((-1, 8, 24), (1, 23, 7)):
        halo(0, dy, wc.at[:, pl.ds(s, 1)], wc.at[:, pl.ds(d, 1)])

    for to, _, c in halos:
        when(to, c.start)
    u_other = pl.ds(pl.multiple_of(other * HALF, HALF), HALF)
    for i, (_, frm, c) in enumerate(halos):
        when(frm, c.wait_recv)

    lane = lax.broadcasted_iota(jnp.int32, (NF, NZ), 1)
    first = lane == 0
    last = lane == NZ - 1

    def row_step(src, su, x, y, ux, uy, wy):
        v = src[x, y]
        u = su[ux, pl.ds(uy, 1), :]
        slope = su[ux + 1, pl.ds(uy, 1), :] - su[ux - 1, pl.ds(uy, 1), :]
        near = src[x, y + 1] + src[x, y - 1]
        near = near + jnp.where(first, 0.0, pltpu.roll(v, 1, 1))
        near = near + jnp.where(last, 0.0, pltpu.roll(v, NZ - 1, 1))
        h = 0.075 * u
        out = (wc[1, pl.ds(wy, 1), :] - 0.075 * slope) * v + 0.15 * near
        out = out + (0.15 - h) * src[x + 1, y] + (0.15 + h) * src[x - 1, y]
        return wc[0, pl.ds(wy, 1), :] * out

    ulane = lax.broadcasted_iota(jnp.int32, (32, NZ), 1)

    def u_step(src, x):
        c = src[x]
        ahead, behind = src[x + 1], src[x - 1]
        near = ahead + behind + pltpu.roll(c, 1, 0) + pltpu.roll(c, 31, 0)
        near = near + jnp.where(ulane == 0, 0.0, pltpu.roll(c, 1, 1))
        near = near + jnp.where(ulane == NZ - 1, 0.0, pltpu.roll(c, NZ - 1, 1))
        return wc[0] * (
            (wc[1] - 0.075 * (ahead - behind)) * c + 0.15 * near + 0.075
        )

    @pl.loop(0, LX + 2)
    def _(x):
        u1[x] = u_step(ue, x + 1)

        @pl.loop(0, LY // 4)
        def _(b):
            for i in range(4):
                y = 1 + b * 4 + i
                v1[x, y] = row_step(fi, ue, x + 1, y + 1, x + 1, y + 7, y + 7)

    @pl.loop(1, LX + 1)
    def _(x):
        for y in (0, LY + 1):
            v1[x, y] = row_step(fi, ue, x + 1, y + 1, x + 1, y + 7, y + 7)

    def plane(x):
        @pl.loop(0, LY // 4)
        def _(b):
            for i in range(4):
                y = b * 4 + i
                w[g, x, y] = row_step(v1, u1, x + 1, y + 1, x + 1, y + 8, y + 8)

    half = LX // 2
    mine = g * half
    theirs = other * half
    sends = []
    for c in range(half):
        plane(mine + c)
        ref = w.at[g, mine + c]
        sends.append(remote(ref, ref, x_send.at[c], x_recv.at[c], partner))
        sends[-1].start()
    for c in range(half):
        plane(theirs + c)

    @pl.loop(0, LX)
    def _(x):
        c = u_step(u1, x + 1)[8:24]
        base_out[x] = jnp.where(g == 0, c[:, :HALF], c[:, HALF:])

    def rows_gram(a, b, x, acc):
        def step(y, acc):
            r = w[a, x, y]
            return tuple(acc[j] + r * w[b, x, y, pl.ds(j, 1), :] for j in range(NF))

        return lax.fori_loop(0, LY, step, acc, unroll=4)

    zeros = tuple(jnp.zeros((NF, NZ), F32) for _ in range(NF))
    own = lax.fori_loop(0, LX, lambda x, acc: rows_gram(g, g, x, acc), zeros)
    col = lax.broadcasted_iota(jnp.int32, (NF, 128), 1)
    part = jnp.zeros((NF, 128), F32)
    for j in range(NF):
        part = jnp.where(col == 8 + 8 * g + j, jnp.sum(own[j], axis=1, keepdims=True), part)
    cross = zeros
    for c in range(half):
        ref = w.at[other, theirs + c]
        remote(ref, ref, x_send.at[c], x_recv.at[c], partner).wait_recv()
        cross = rows_gram(1, 0, theirs + c, cross)
    for j in range(NF):
        part = jnp.where(col == j, jnp.sum(cross[j], axis=1, keepdims=True), part)
    me = g * GY + gy
    tile[0] = part
    al[me] = part

    def p_copy(off):
        dev = (1, gx, lax.rem(gy + off, GY))
        return remote(tile.at[0], al.at[me], p_send.at[off], p_recv.at[me], dev)

    for off in P_ORDER:
        when(g == 0 if off == 0 else None, p_copy(off).start)

    tail_ref = w.at[0, pl.ds(half, half)]
    tail = remote(tail_ref, tail_ref, x_send.at[half], x_recv.at[half], (1, gx, gy))
    final = remote(gs, gs, x_send.at[half + 1], x_recv.at[half + 1], (0, gx, gy))

    @pl.when(g == 0)
    def _():
        tail.start()
        final.wait_recv()

    def z_copy(off):
        dev = (1, lax.rem(gx + off, GX), gy)
        return remote(tile.at[1], zl.at[gx], z_send.at[off], z_recv.at[gx], dev)

    @pl.when(g == 1)
    def _():
        for s in range(2 * GY):
            c = remote(tile.at[0], al.at[s], p_send.at[0], p_recv.at[s], partner)
            when(None if s < GY else gy != s - GY, c.wait_recv)
        total = al[0]
        for s in range(1, 2 * GY):
            total = total + al[s]
        tile[1] = total
        zl[gx] = total
        for off in Z_ORDER:
            z_copy(off).start()
        for s in range(GX):
            c = remote(tile.at[1], zl.at[s], z_send.at[0], z_recv.at[s], partner)
            when(gx != s, c.wait_recv)
        total = zl[0]
        for s in range(1, GX):
            total = total + zl[s]
        gs[...] = total * (1.0 / CELLS)
        final.start()

    gram = gs[...]
    sub8 = lax.broadcasted_iota(jnp.int32, (NF, 128), 0)
    g01 = jnp.zeros((NF, 128), F32)
    for j in range(NF):
        row = jnp.where(col == sub8, gram[j : j + 1, :], 0.0)
        g01 = jnp.where(col == 8 + j, jnp.sum(row, axis=1, keepdims=True), g01)
    shifted = pltpu.roll(gram, 120, 1)
    top = jnp.where(col < 8, shifted, g01)
    low = jnp.where(col < 8, gram, shifted)
    top = jnp.where(col < 16, top, jnp.where(col == 16 + sub8, 1.0, 0.0))
    low = jnp.where(col < 16, low, jnp.where(col == 24 + sub8, 1.0, 0.0))
    m = jnp.concatenate([top, low], axis=0)
    sub = lax.broadcasted_iota(jnp.int32, (2 * NF, 128), 0)
    col16 = lax.broadcasted_iota(jnp.int32, (2 * NF, 128), 1)
    for k in range(2 * NF - 1):
        pivot = m[k : k + 1, :]
        factor = m[:, k : k + 1] / pivot[:, k : k + 1]
        m = m - jnp.where(sub > k, factor, 0.0) * pivot
    diag = jnp.where(col16 == sub, m, 0.0)
    root_row = jnp.sqrt(jnp.sum(diag, axis=0, keepdims=True))
    root_col = jnp.sqrt(jnp.sum(diag, axis=1, keepdims=True))
    growth_out[...] = jnp.log(root_row)[:, :16]
    inv = m / root_col

    def emit(groups, rows):
        cols = [
            jnp.broadcast_to(rows[:, 16 + j : 17 + j], (NF, NZ)) for j in range(NF * groups)
        ]

        def step(x, carry):
            def inner(y, carry):
                acc = None
                for b in range(groups):
                    for j in range(NF):
                        t = cols[b * NF + j] * w[b, x, y, pl.ds(j, 1), :]
                        acc = t if acc is None else acc + t
                o[x, y] = acc
                return carry

            return lax.fori_loop(0, LY, inner, carry, unroll=4)

        for part_ in range(2):
            lax.fori_loop(part_ * half, part_ * half + half, step, 0)
            for f in range(NF):
                out_copy(part_, f).start()

    def out_copy(part_, f):
        r = pl.ds(part_ * half, half)
        return pltpu.make_async_copy(
            o.at[r, :, f], ortho_hbm.at[f, r], out_sem.at[part_ * NF + f]
        )

    @pl.when(g == 0)
    def _():
        emit(1, inv[:NF])

    @pl.when(g == 1)
    def _():
        tail.wait_recv()
        emit(2, inv[NF:])

    for part_ in range(2):
        for f in range(NF):
            out_copy(part_, f).wait()
    for to, _, c in halos:
        when(to, c.wait_send)
    for c in sends:
        c.wait_send()
    for off in P_ORDER:
        when(g == 0 if off == 0 else None, p_copy(off).wait_send)

    @pl.when(g == 0)
    def _():
        tail.wait_send()

    @pl.when(g == 1)
    def _():
        final.wait_send()
        for off in Z_ORDER:
            z_copy(off).wait_send()


def body(base_flow, fields, wall_mask, conduct_flag):
    vmem = pl.BlockSpec(memory_space=pltpu.VMEM)
    hbm = pl.BlockSpec(memory_space=pl.ANY)
    dma = pltpu.SemaphoreType.DMA
    base, ortho, growth = pl.pallas_call(
        kernel,
        out_shape=[
            jax.ShapeDtypeStruct(base_flow.shape, F32),
            jax.ShapeDtypeStruct(fields.shape, F32),
            jax.ShapeDtypeStruct((1, 2 * NF), F32),
        ],
        in_specs=[hbm, hbm, vmem, vmem],
        out_specs=[vmem, hbm, vmem],
        scratch_shapes=[
            pltpu.VMEM((LX + 4, LY + 4, NF, NZ), F32),
            pltpu.VMEM((LX + 2, LY + 2, NF, NZ), F32),
            pltpu.VMEM((2, LX, LY, NF, NZ), F32),
            pltpu.VMEM((LX, LY, NF, NZ), F32),
            pltpu.VMEM((LX + 4, 32, NZ), F32),
            pltpu.VMEM((LX + 2, 32, NZ), F32),
            pltpu.VMEM((2, 32, NZ), F32),
            pltpu.VMEM((2, NF, 128), F32),
            pltpu.VMEM((2 * GY, NF, 128), F32),
            pltpu.VMEM((GX, NF, 128), F32),
            pltpu.VMEM((NF, 128), F32),
            dma((NF + 1,)),
            dma((2 * NF,)),
            dma((32,)),
            dma((32,)),
            dma((6,)),
            dma((6,)),
            dma((GY,)),
            dma((2 * GY,)),
            dma((GX,)),
            dma((GX,)),
        ],
        compiler_params=pltpu.CompilerParams(
            collective_id=0, has_side_effects=True, vmem_limit_bytes=24 << 20
        ),
    )(base_flow, fields, wall_mask, conduct_flag)
    return base, ortho, growth.reshape(2 * NF)


def solution(mesh):
    in_specs = (P("gx", "gy", "grp"), P("grp", "gx", "gy", None), P("gy", None), P("gy", None))
    out_specs = (P("gx", "gy", "grp"), P("grp", "gx", "gy", None), P())
    return jax.shard_map(body, mesh=mesh, in_specs=in_specs, out_specs=out_specs, check_vma=False)
```

time: 225 us -> 63.5 us (0.28)
  blocking collectives: 95.9 us -> 0 us
  Pallas kernels: 0 us -> 56.9 us
  starting transfers between devices: 32.6 us -> 0 us
  local copies, waits for them, and re-layouts: 35.6 us -> 5.6 us
  waiting for transfers between devices: 27.4 us -> 0 us
  other arithmetic: 26.7 us -> 0 us
  matrix products: 4.47 us -> 0 us
    psum x1 -> x0, blocking collectives: 87.3 us -> none  [body(): gram = lax.psum(partial_gram, ('grp', 'gx', 'gy')) / float(total_cells)]
    pallas_call x0 -> x1, Pallas kernels: none -> 56.9 us  [body(): pl.pallas_call(kernel, out_shape=[jax.ShapeDtypeStruct(base_flow.shape, F...]
    ppermute x8 -> x0, starting transfers between devices: 25.3 us -> none  [the longest x4 13.6 us: with_halo(): lax.ppermute(lax.slice_in_dim(block, 0, width, axis=dim), axis, backward)]
    all_to_all x2 -> x0, waiting for transfers between devices: 19.2 us -> none  [the longest x1 10.4 us: body(): lax.all_to_all(renormed, 'grp', split_axis=0, concat_axis=3, tiled=True)]
    all_to_all x3 -> x0, local copies, waits for them, and re-layouts: 9 us -> none  [the longest x2 7.89 us: body(): lax.all_to_all(working, 'grp', split_axis=3, concat_axis=0, tiled=True)]
    all_gather x2 -> x0, blocking collectives: 8.55 us -> none  [body(): whole = lax.all_gather(base, 'grp', axis=2, tiled=True)]
    unnamed x21 -> x11, local copies, waits for them, and re-layouts: 13.8 us -> 5.6 us
    ppermute x8 -> x0, waiting for transfers between devices: 8.15 us -> none  [the longest x4 4.64 us: with_halo(): lax.ppermute(lax.slice_in_dim(block, block.shape[dim] - width, None, axis...]
  transfers between devices with their start and end apart: 10 -> 0, of which waited for: 8 -> 0; matrix products, arithmetic and copies ran while one was open for 1% -> 0% of each run, Pallas kernels for 0% -> 0%
where the time goes in v1:
time: 63.5 us; the launch traced here: 63.2 us
  Pallas kernels  56.9 us (90%)
  local copies, waits for them, and re-layouts  5.6 us (9%)
  between operations  0.65 us (1%)
    pallas_call x1, Pallas kernels, body(): pl.pallas_call(kernel, out_shape=[jax.ShapeDtypeStruct(base_flow.shape, F...  56.9 us
    unnamed x11, local copies, waits for them, and re-layouts  5.6 us

profile of v1, /device:TPU:1, one launch (start us, length us, event | category | flops | bytes accessed | tf_op | source)
XLA Modules:
  0.0 63.2 jit_solution(13598166631885281565)
XLA Ops:
  0.6 0.0 copy-start
  0.6 1.2 %copy-done = f32[8,8,16,256]{3,2,1,0:T(8,128)S(1)} copy-done((f32[8,8,16,256]{3,2,1,0:T(8,128)S(1)}, f32[8,8,16,256]{3,2,1,0:T(8,128)}, u32[]{:S(2)}) %copy-start) | copy-done | bytes 1048600
  1.9 0.0 copy-start.1
  1.9 0.8 %copy-done.1 = f32[8,16,128]{2,1,0:T(8,128)S(1)} copy-done((f32[8,16,128]{2,1,0:T(8,128)S(1)}, f32[8,16,128]{2,1,0:T(8,128)}, u32[]{:S(2)}) %copy-start.1) | copy-done | bytes 65560
  2.7 0.0 copy-start.2
  2.7 0.7 %copy-done.2 = s32[16,256]{1,0:T(8,128)S(1)} copy-done((s32[16,256]{1,0:T(8,128)S(1)}, s32[16,256]{1,0:T(8,128)}, u32[]{:S(2)}) %copy-start.2) | copy-done | bytes 16408
  3.4 0.0 copy-start.3
  3.4 0.7 %copy-done.3 = s32[16,256]{1,0:T(8,128)S(1)} copy-done((s32[16,256]{1,0:T(8,128)S(1)}, s32[16,256]{1,0:T(8,128)}, u32[]{:S(2)}) %copy-start.3) | copy-done | bytes 16408
  4.1 56.9 %shard_map.67 = (f32[8,16,128]{2,1,0:T(8,128)S(1)}, f32[8,8,16,256]{3,2,1,0:T(8,128)S(1)}, f32[1,16]{1,0:T(1,128)S(1)}) custom-call(f32[8,16,128]{2,1,0:T(8,128)S(1)} %copy-done.1, f32[8,8,16,256]{3,2,1,0:T(8,128)S(1)} %copy-done, s32[16,256]{1,0:T(8,128)S(1)} %copy-done.2, s32[16,256]{1,0:T(8,128)S(1)} %copy-done.3), custom_call_target="tpu_custom_call" | custom-call | tf_op jit(solution)/shard_map/pallas_call | solution.py:373
  61.1 0.6 %copy.10 = f32[8,16,128]{2,1,0:T(8,128)} copy(f32[8,16,128]{2,1,0:T(8,128)S(1)} %get-tuple-element.12) | data formatting | bytes 131072
  61.7 1.0 %copy.11 = f32[8,8,16,256]{3,2,1,0:T(8,128)} copy(f32[8,8,16,256]{3,2,1,0:T(8,128)S(1)} %get-tuple-element.13) | data formatting | bytes 2097152
  62.7 0.5 copy.12
Async XLA Ops:
  0.6 1.2 %copy-start = (f32[8,8,16,256]{3,2,1,0:T(8,128)S(1)}, f32[8,8,16,256]{3,2,1,0:T(8,128)}, u32[]{:S(2)}) copy-start(f32[8,8,16,256]{3,2,1,0:T(8,128)} %fields_hbm.1) | copy-start | bytes 3145732
  1.9 0.8 %copy-start.1 = (f32[8,16,128]{2,1,0:T(8,128)S(1)}, f32[8,16,128]{2,1,0:T(8,128)}, u32[]{:S(2)}) copy-start(f32[8,16,128]{2,1,0:T(8,128)} %base_hbm.1) | copy-start | bytes 196612
  2.7 0.7 %copy-start.2 = (s32[16,256]{1,0:T(8,128)S(1)}, s32[16,256]{1,0:T(8,128)}, u32[]{:S(2)}) copy-start(s32[16,256]{1,0:T(8,128)} %wall_ref.1) | copy-start | bytes 49156
  3.4 0.7 %copy-start.3 = (s32[16,256]{1,0:T(8,128)S(1)}, s32[16,256]{1,0:T(8,128)}, u32[]{:S(2)}) copy-start(s32[16,256]{1,0:T(8,128)} %cond_ref.1) | copy-start | bytes 49156

commit v2 on v1

--- a/solution.py
+++ b/solution.py
@@ -42,10 +42,10 @@
 
 
 def kernel(
-    base_hbm, fields_hbm, wall_ref, cond_ref,
-    base_out, ortho_hbm, growth_out,
-    fi, v1, w, o, ue, u1, wc, tile, al, zl, gs,
-    ld_sem, out_sem, h_send, h_recv, x_send, x_recv, p_send, p_recv, z_send, z_recv,
+    base_hbm, fields_hbm, wall_hbm, cond_hbm,
+    w, base_out, coef_out, growth_out,
+    fi, v1, ue, u1, masks, wc, tile, al, zl, gs,
+    ld_sem, h_send, h_recv, x_send, x_recv, p_send, p_recv, z_send, z_recv,
 ):
     g = lax.axis_index("grp")
     gx = lax.axis_index("gx")
@@ -58,13 +58,17 @@
 
     loads = [
         pltpu.make_async_copy(
+            base_hbm, ue.at[pl.ds(2, LX), pl.ds(8, LY), lanes], ld_sem.at[NF]
+        ),
+        pltpu.make_async_copy(wall_hbm, masks.at[0], ld_sem.at[NF + 1]),
+        pltpu.make_async_copy(cond_hbm, masks.at[1], ld_sem.at[NF + 2]),
+    ]
+    loads += [
+        pltpu.make_async_copy(
             fields_hbm.at[f], fi.at[pl.ds(2, LX), pl.ds(2, LY), f], ld_sem.at[f]
         )
         for f in range(NF)
     ]
-    loads.append(
-        pltpu.make_async_copy(base_hbm, ue.at[pl.ds(2, LX), pl.ds(8, LY), lanes], ld_sem.at[NF])
-    )
     for c in loads:
         c.start()
 
@@ -94,9 +98,6 @@
         )
         count = count + (1 if ok is None else jnp.where(ok, 1, 0))
 
-    wc[0, pl.ds(8, LY), :] = wall_ref[...].astype(F32)
-    wc[1, pl.ds(8, LY), :] = 0.1 - 0.15 * (0.25 * (1.0 + 3.0 * cond_ref[...].astype(F32)))
-
     for ok, row, urow, wrow in ((gy == 0, 0, 6, 7), (gy == GY - 1, LY + 2, 24, 24)):
 
         def clear(row=row, urow=urow, wrow=wrow):
@@ -110,6 +111,8 @@
 
     for c in loads:
         c.wait()
+    wc[0, pl.ds(8, LY), :] = masks[0].astype(F32)
+    wc[1, pl.ds(8, LY), :] = 0.1 - 0.15 * (0.25 * (1.0 + 3.0 * masks[1].astype(F32)))
     pl.semaphore_wait(barrier, count)
 
     halos = []
@@ -123,34 +126,36 @@
 
     xs, ys = pl.ds(2, LX), pl.ds(2, LY)
     yu = pl.ds(8, LY)
-    for dy, src, dst in ((-1, 2, LY + 2), (1, LY, 0)):
-        halo(0, dy, fi.at[xs, pl.ds(src, 2)], fi.at[xs, pl.ds(dst, 2)])
-    for dx, src, dst in ((-1, 2, LX + 2), (1, LX, 0)):
-        halo(dx, 0, fi.at[pl.ds(src, 2), ys], fi.at[pl.ds(dst, 2), ys])
     src = ue.at[xs, yu, lanes]
     halo(0, 0, src, src, other)
-    for who in (None, other):
-        for dy, s, d in ((-1, 8, 24), (1, 22, 6)):
-            halo(0, dy, ue.at[xs, pl.ds(s, 2), lanes], ue.at[xs, pl.ds(d, 2), lanes], who)
-        for dx, s, d in ((-1, 2, LX + 2), (1, LX, 0)):
-            halo(dx, 0, ue.at[pl.ds(s, 2), yu, lanes], ue.at[pl.ds(d, 2), yu, lanes], who)
+    for who in (other, None):
         for dx, sx, tx in ((-1, 2, LX + 2), (1, LX + 1, 1)):
             for dy, sy, ty in ((-1, 8, 24), (1, 23, 7)):
                 halo(
                     dx, dy,
                     ue.at[sx, pl.ds(sy, 1), lanes], ue.at[tx, pl.ds(ty, 1), lanes], who,
                 )
+        for dy, s, d in ((-1, 8, 24), (1, 22, 6)):
+            halo(0, dy, ue.at[xs, pl.ds(s, 2), lanes], ue.at[xs, pl.ds(d, 2), lanes], who)
+        for dx, s, d in ((-1, 2, LX + 2), (1, LX, 0)):
+            halo(dx, 0, ue.at[pl.ds(s, 2), yu, lanes], ue.at[pl.ds(d, 2), yu, lanes], who)
+    for dy, s, d in ((-1, 8, 24), (1, 23, 7)):
+        halo(0, dy, wc.at[:, pl.ds(s, 1)], wc.at[:, pl.ds(d, 1)])
+    u_count = len(halos)
+    for dx, src, dst in ((-1, 2, LX + 2), (1, LX, 0)):
+        halo(dx, 0, fi.at[pl.ds(src, 2), ys], fi.at[pl.ds(dst, 2), ys])
+    for dy, src, dst in ((-1, 2, LY + 2), (1, LY, 0)):
+        halo(0, dy, fi.at[xs, pl.ds(src, 2)], fi.at[xs, pl.ds(dst, 2)])
     for dx, sx, tx in ((-1, 2, LX + 2), (1, LX + 1, 1)):
         for dy, sy, ty in ((-1, 2, LY + 2), (1, LY + 1, 1)):
             halo(dx, dy, fi.at[sx, sy], fi.at[tx, ty])
-    for dy, s, d in ((-1, 8, 24), (1, 23, 7)):
-        halo(0, dy, wc.at[:, pl.ds(s, 1)], wc.at[:, pl.ds(d, 1)])
 
     for to, _, c in halos:
         when(to, c.start)
-    u_other = pl.ds(pl.multiple_of(other * HALF, HALF), HALF)
-    for i, (_, frm, c) in enumerate(halos):
-        when(frm, c.wait_recv)
+
+    def arrive(lo, hi):
+        for _, frm, c in halos[lo:hi]:
+            when(frm, c.wait_recv)
 
     lane = lax.broadcasted_iota(jnp.int32, (NF, NZ), 1)
     first = lane == 0
@@ -180,63 +185,120 @@
             (wc[1] - 0.075 * (ahead - behind)) * c + 0.15 * near + 0.075
         )
 
+    def first_rows(x, rows):
+        for y in rows:
+            v1[x, y] = row_step(fi, ue, x + 1, y + 1, x + 1, y + 7, y + 7)
+
+    def second_rows(x, rows):
+        for y in rows:
+            w[g, x, y] = row_step(v1, u1, x + 1, y + 1, x + 1, y + 8, y + 8)
+
+    def first_inner(x):
+        @pl.loop(0, 2)
+        def _(b):
+            first_rows(x, [2 + b * 7 + i for i in range(7)])
+
+    def second_inner(x):
+        @pl.loop(0, 2)
+        def _(b):
+            second_rows(x, [2 + b * 6 + i for i in range(6)])
+
+    half = LX // 2
+    inner = pl.ds(2, LY - 4)
+    edges = (pl.ds(0, 2), pl.ds(LY - 2, 2))
+
+    def pieces(s):
+        near = [w.at[s, 2 + 2 * s + i, inner] for i in range(2)]
+        far = [w.at[s, 6 * s + i, inner] for i in range(2)]
+        rim = [w.at[s, pl.ds(half * s, half), e] for e in edges]
+        return near + far + rim
+
+    sends = [
+        remote(r, r, x_send.at[i], x_recv.at[i], partner) for i, r in enumerate(pieces(g))
+    ]
+    gets = [
+        remote(r, r, x_send.at[i], x_recv.at[i], partner)
+        for i, r in enumerate(pieces(other))
+    ]
+
+    arrive(0, u_count)
+
     @pl.loop(0, LX + 2)
     def _(x):
         u1[x] = u_step(ue, x + 1)
 
-        @pl.loop(0, LY // 4)
-        def _(b):
-            for i in range(4):
-                y = 1 + b * 4 + i
-                v1[x, y] = row_step(fi, ue, x + 1, y + 1, x + 1, y + 7, y + 7)
+    @pl.loop(0, 4)
+    def _(i):
+        first_inner(2 + 2 * g + i)
+
+    for i in range(2):
+        second_inner(2 + 2 * g + i)
+        sends[i].start()
+
+    arrive(u_count, u_count + 2)
+    for i in range(2):
+        first_inner(8 * g + i)
+    for i in range(2):
+        second_inner(6 * g + i)
+        sends[2 + i].start()
+
+    @pl.loop(0, 4)
+    def _(i):
+        first_inner(6 * other + i)
+
+    arrive(u_count + 2, len(halos))
+
+    @pl.loop(0, LX + 2)
+    def _(x):
+        first_rows(x, (1, LY))
 
     @pl.loop(1, LX + 1)
     def _(x):
-        for y in (0, LY + 1):
-            v1[x, y] = row_step(fi, ue, x + 1, y + 1, x + 1, y + 7, y + 7)
-
-    def plane(x):
-        @pl.loop(0, LY // 4)
-        def _(b):
-            for i in range(4):
-                y = b * 4 + i
-                w[g, x, y] = row_step(v1, u1, x + 1, y + 1, x + 1, y + 8, y + 8)
-
-    half = LX // 2
-    mine = g * half
-    theirs = other * half
-    sends = []
-    for c in range(half):
-        plane(mine + c)
-        ref = w.at[g, mine + c]
-        sends.append(remote(ref, ref, x_send.at[c], x_recv.at[c], partner))
-        sends[-1].start()
-    for c in range(half):
-        plane(theirs + c)
+        first_rows(x, (0, LY + 1))
+
+    for e in range(2):
+
+        @pl.loop(0, half)
+        def _(x, e=e):
+            second_rows(half * g + x, (0, 1) if e == 0 else (LY - 2, LY - 1))
+
+        sends[4 + e].start()
+
+    @pl.loop(0, half)
+    def _(x):
+        second_inner(half * other + x)
+        second_rows(half * other + x, (0, 1, LY - 2, LY - 1))
 
     @pl.loop(0, LX)
     def _(x):
         c = u_step(u1, x + 1)[8:24]
         base_out[x] = jnp.where(g == 0, c[:, :HALF], c[:, HALF:])
 
-    def rows_gram(a, b, x, acc):
+    def gram_rows(a, b, x, lo, n, acc, unroll):
         def step(y, acc):
             r = w[a, x, y]
             return tuple(acc[j] + r * w[b, x, y, pl.ds(j, 1), :] for j in range(NF))
 
-        return lax.fori_loop(0, LY, step, acc, unroll=4)
+        return lax.fori_loop(lo, lo + n, step, acc, unroll=unroll)
 
     zeros = tuple(jnp.zeros((NF, NZ), F32) for _ in range(NF))
-    own = lax.fori_loop(0, LX, lambda x, acc: rows_gram(g, g, x, acc), zeros)
+    own = lax.fori_loop(0, LX, lambda x, acc: gram_rows(g, g, x, 0, LY, acc, 4), zeros)
     col = lax.broadcasted_iota(jnp.int32, (NF, 128), 1)
     part = jnp.zeros((NF, 128), F32)
     for j in range(NF):
         part = jnp.where(col == 8 + 8 * g + j, jnp.sum(own[j], axis=1, keepdims=True), part)
     cross = zeros
-    for c in range(half):
-        ref = w.at[other, theirs + c]
-        remote(ref, ref, x_send.at[c], x_recv.at[c], partner).wait_recv()
-        cross = rows_gram(1, 0, theirs + c, cross)
+    for i in range(4):
+        gets[i].wait_recv()
+        x = (2 + 2 * other if i < 2 else 6 * other) + i % 2
+        cross = gram_rows(1, 0, x, 2, LY - 4, cross, 4)
+    for e in range(2):
+        gets[4 + e].wait_recv()
+        cross = lax.fori_loop(
+            0, half,
+            lambda x, acc: gram_rows(1, 0, half * other + x, e * (LY - 2), 2, acc, 2),
+            cross,
+        )
     for j in range(NF):
         part = jnp.where(col == j, jnp.sum(cross[j], axis=1, keepdims=True), part)
     me = g * GY + gy
@@ -251,8 +313,8 @@
         when(g == 0 if off == 0 else None, p_copy(off).start)
 
     tail_ref = w.at[0, pl.ds(half, half)]
-    tail = remote(tail_ref, tail_ref, x_send.at[half], x_recv.at[half], (1, gx, gy))
-    final = remote(gs, gs, x_send.at[half + 1], x_recv.at[half + 1], (0, gx, gy))
+    tail = remote(tail_ref, tail_ref, x_send.at[6], x_recv.at[6], (1, gx, gy))
+    final = remote(gs, gs, x_send.at[7], x_recv.at[7], (0, gx, gy))
 
     @pl.when(g == 0)
     def _():
@@ -307,14 +369,55 @@
     root_col = jnp.sqrt(jnp.sum(diag, axis=1, keepdims=True))
     growth_out[...] = jnp.log(root_row)[:, :16]
     inv = m / root_col
-
-    def emit(groups, rows):
+    coef_out[...] = jnp.where(g == 0, inv[:NF], inv[NF:])
+
+    @pl.when(g == 1)
+    def _():
+        tail.wait_recv()
+
+    for to, _, c in halos:
+        when(to, c.wait_send)
+    for c in sends:
+        c.wait_send()
+    for off in P_ORDER:
+        when(g == 0 if off == 0 else None, p_copy(off).wait_send)
+
+    @pl.when(g == 0)
+    def _():
+        tail.wait_send()
+
+    @pl.when(g == 1)
+    def _():
+        final.wait_send()
+        for off in Z_ORDER:
+            z_copy(off).wait_send()
+
+
+def apply_kernel(
+    w, base, coef, growth, base_hbm, ortho_hbm, growth_hbm, o, out_sem
+):
+    g = lax.axis_index("grp")
+    small = [
+        pltpu.make_async_copy(base, base_hbm, out_sem.at[4 * NF]),
+        pltpu.make_async_copy(growth, growth_hbm, out_sem.at[4 * NF + 1]),
+    ]
+    for c in small:
+        c.start()
+    step = LX // 4
+
+    def out_copy(q, f):
+        r = pl.ds(q * step, step)
+        return pltpu.make_async_copy(
+            o.at[r, :, f], ortho_hbm.at[f, r], out_sem.at[q * NF + f]
+        )
+
+    def emit(groups):
         cols = [
-            jnp.broadcast_to(rows[:, 16 + j : 17 + j], (NF, NZ)) for j in range(NF * groups)
+            jnp.broadcast_to(coef[:, 16 + j : 17 + j], (NF, NZ)) for j in range(NF * groups)
         ]
 
-        def step(x, carry):
-            def inner(y, carry):
+        def plane(x, carry):
+            def row(y, carry):
                 acc = None
                 for b in range(groups):
                     for j in range(NF):
@@ -323,89 +426,80 @@
                 o[x, y] = acc
                 return carry
 
-            return lax.fori_loop(0, LY, inner, carry, unroll=4)
-
-        for part_ in range(2):
-            lax.fori_loop(part_ * half, part_ * half + half, step, 0)
+            return lax.fori_loop(0, LY, row, carry, unroll=4)
+
+        for q in range(4):
+            lax.fori_loop(q * step, (q + 1) * step, plane, 0)
             for f in range(NF):
-                out_copy(part_, f).start()
-
-    def out_copy(part_, f):
-        r = pl.ds(part_ * half, half)
-        return pltpu.make_async_copy(
-            o.at[r, :, f], ortho_hbm.at[f, r], out_sem.at[part_ * NF + f]
-        )
+                out_copy(q, f).start()
 
     @pl.when(g == 0)
     def _():
-        emit(1, inv[:NF])
+        emit(1)
 
     @pl.when(g == 1)
     def _():
-        tail.wait_recv()
-        emit(2, inv[NF:])
-
-    for part_ in range(2):
+        emit(2)
+
+    for q in range(4):
         for f in range(NF):
-            out_copy(part_, f).wait()
-    for to, _, c in halos:
-        when(to, c.wait_send)
-    for c in sends:
-        c.wait_send()
-    for off in P_ORDER:
-        when(g == 0 if off == 0 else None, p_copy(off).wait_send)
-
-    @pl.when(g == 0)
-    def _():
-        tail.wait_send()
-
-    @pl.when(g == 1)
-    def _():
-        final.wait_send()
-        for off in Z_ORDER:
-            z_copy(off).wait_send()
-
-
-def body(base_flow, fields, wall_mask, conduct_flag):
+            out_copy(q, f).wait()
+    for c in small:
+        c.wait()
+
+
+def body(*arrays):
+    base_flow, fields = arrays[:2]
     vmem = pl.BlockSpec(memory_space=pltpu.VMEM)
-    hbm = pl.BlockSpec(memory_space=pl.ANY)
+    hbm = pl.BlockSpec(memory_space=pltpu.HBM)
     dma = pltpu.SemaphoreType.DMA
-    base, ortho, growth = pl.pallas_call(
+    stepped, base, coef, growth = pl.pallas_call(
         kernel,
         out_shape=[
-            jax.ShapeDtypeStruct(base_flow.shape, F32),
-            jax.ShapeDtypeStruct(fields.shape, F32),
-            jax.ShapeDtypeStruct((1, 2 * NF), F32),
+            pltpu.VMEM((2, LX, LY, NF, NZ), F32),
+            pltpu.VMEM(base_flow.shape, F32),
+            pltpu.VMEM((NF, 128), F32),
+            pltpu.VMEM((1, 2 * NF), F32),
         ],
-        in_specs=[hbm, hbm, vmem, vmem],
-        out_specs=[vmem, hbm, vmem],
+        in_specs=[hbm] * 4,
+        out_specs=[vmem] * 4,
         scratch_shapes=[
             pltpu.VMEM((LX + 4, LY + 4, NF, NZ), F32),
             pltpu.VMEM((LX + 2, LY + 2, NF, NZ), F32),
-            pltpu.VMEM((2, LX, LY, NF, NZ), F32),
-            pltpu.VMEM((LX, LY, NF, NZ), F32),
             pltpu.VMEM((LX + 4, 32, NZ), F32),
             pltpu.VMEM((LX + 2, 32, NZ), F32),
+            pltpu.VMEM((2, LY, NZ), jnp.int32),
             pltpu.VMEM((2, 32, NZ), F32),
             pltpu.VMEM((2, NF, 128), F32),
             pltpu.VMEM((2 * GY, NF, 128), F32),
             pltpu.VMEM((GX, NF, 128), F32),
             pltpu.VMEM((NF, 128), F32),
-            dma((NF + 1,)),
-            dma((2 * NF,)),
+            dma((NF + 3,)),
             dma((32,)),
             dma((32,)),
-            dma((6,)),
-            dma((6,)),
+            dma((8,)),
+            dma((8,)),
             dma((GY,)),
             dma((2 * GY,)),
             dma((GX,)),
             dma((GX,)),
         ],
         compiler_params=pltpu.CompilerParams(
-            collective_id=0, has_side_effects=True, vmem_limit_bytes=24 << 20
+            collective_id=0, has_side_effects=True, vmem_limit_bytes=16 << 20
         ),
-    )(base_flow, fields, wall_mask, conduct_flag)
+    )(*(pltpu.with_memory_space_constraint(a, pltpu.HBM) for a in arrays))
+    base, ortho, growth = pl.pallas_call(
+        apply_kernel,
+        out_shape=[
+            jax.ShapeDtypeStruct(base_flow.shape, F32),
+            jax.ShapeDtypeStruct(fields.shape, F32),
+            jax.ShapeDtypeStruct((1, 2 * NF), F32),
+        ],
+        in_specs=[vmem] * 4,
+        out_specs=[hbm] * 3,
+        scratch_shapes=[pltpu.VMEM((LX, LY, NF, NZ), F32), dma((4 * NF + 2,))],
+        compiler_params=pltpu.CompilerParams(vmem_limit_bytes=16 << 20),
+    )(stepped, base, coef, growth)
     return base, ortho, growth.reshape(2 * NF)
 
 

time: 63.5 us -> 50.4 us (0.79)
  Pallas kernels: 56.9 us -> 49.3 us
  local copies, waits for them, and re-layouts: 5.6 us -> 0 us
    pallas_call x1 -> x2, Pallas kernels: 56.9 us -> 49.3 us  [the longest x1 47.3 us: body(): pl.pallas_call(kernel, out_shape=[pltpu.VMEM((2, LX, LY, NF, NZ), F32), p...]
    unnamed x11 -> x0, local copies, waits for them, and re-layouts: 5.6 us -> none
where the time goes in v2:
time: 50.4 us; the launch traced here: 49.9 us
  Pallas kernels  49.3 us (98%)
  between operations  0.64 us (1%)
    pallas_call x1, Pallas kernels, body(): pl.pallas_call(kernel, out_shape=[pltpu.VMEM((2, LX, LY, NF, NZ), F32), p...  47.3 us
    pallas_call x1, Pallas kernels, body(): pl.pallas_call(apply_kernel, out_shape=[jax.ShapeDtypeStruct(base_flow.sh...  2.02 us

profile of v2, /device:TPU:1, one launch (start us, length us, event | category | flops | bytes accessed | tf_op | source)
XLA Modules:
  0.0 49.9 jit_solution(10024650201796398348)
XLA Ops:
  0.6 47.3 %shard_map.67 = (f32[2,8,16,8,256]{4,3,2,1,0:T(8,128)S(1)}, f32[8,16,128]{2,1,0:T(8,128)S(1)}, f32[8,128]{1,0:T(8,128)S(1)}, f32[1,16]{1,0:T(1,128)S(1)}) custom-call(f32[8,16,128]{2,1,0:T(8,128)} %base_hbm.1, f32[8,8,16,256]{3,2,1,0:T(8,128)} %fields_hbm.1, s32[16,256]{1,0:T(8,128)} %wall_hbm.1, s32[16,256]{1,0:T(8,128)} %cond_hbm.1), custom_call_target="tpu_custom_call" | custom-call | tf_op jit(solution)/shard_map/pallas_call | solution.py:456
  47.9 2.0 %shard_map.68 = (f32[8,16,128]{2,1,0:T(8,128)}, f32[8,8,16,256]{3,2,1,0:T(8,128)}, f32[1,16]{1,0:T(1,128)}) custom-call(f32[2,8,16,8,256]{4,3,2,1,0:T(8,128)S(1)} %get-tuple-element.10.w, f32[8,16,128]{2,1,0:T(8,128)S(1)} %get-tuple-element.11.base, f32[8,128]{1,0:T(8,128)S(1)} %get-tuple-element.12.coef, f32[1,16]{1,0:T(1,128)S(1)} %get-tuple-element.13.growth), custom_call_target="tpu_custom_call" | custom-call | tf_op jit(solution)/shard_map/pallas_call | solution.py:491

commit v3 on v2

--- a/solution.py
+++ b/solution.py
@@ -10,8 +10,10 @@
 GX, GY = 16, 8
 LX, LY, NF, NZ = 8, 16, 8, 256
 HALF = NZ // 2
+PARTS = 2
 CELLS = 4194304.0
-P_ORDER = (4, 3, 5, 2, 6, 1, 7, 0)
+P_ORDER = tuple((off, swap) for off in (4, 3, 5, 2, 6, 1, 7, 0) for swap in (1, 0) if off or swap)
+TAIL = ((4, 2), (6, 2))
 Z_ORDER = (8, 7, 9, 6, 10, 5, 11, 4, 12, 3, 13, 2, 14, 1, 15)
 
 
@@ -33,18 +35,10 @@
     )
 
 
-def both(*conds):
-    out = None
-    for c in conds:
-        if c is not None:
-            out = c if out is None else jnp.logical_and(out, c)
-    return out
-
-
 def kernel(
     base_hbm, fields_hbm, wall_hbm, cond_hbm,
     w, base_out, coef_out, growth_out,
-    fi, v1, ue, u1, masks, wc, tile, al, zl, gs,
+    fi, v1, ue, u1, masks, wc, tile, al, zl,
     ld_sem, h_send, h_recv, x_send, x_recv, p_send, p_recv, z_send, z_recv,
 ):
     g = lax.axis_index("grp")
@@ -55,6 +49,27 @@
     has_low = gy > 0
     has_high = gy < GY - 1
     lanes = pl.ds(pl.multiple_of(g * HALF, HALF), HALF)
+
+    barrier = pltpu.get_barrier_semaphore()
+    count = 0
+    greet = []
+    for dy in (-1, 1, 0):
+        for dx in (0, -1, 1):
+            for side in (0, 1):
+                if dx == 0 and dy == 0 and side == 0:
+                    continue
+                ok = None if dy == 0 else (has_low if dy < 0 else has_high)
+                who = g if side == 0 else other
+                greet.append((ok, (who, lax.rem(gx + dx + GX, GX), gy + dy)))
+    def signal(ok, dev):
+        when(
+            ok,
+            lambda: pl.semaphore_signal(barrier, inc=1, device_id=dev, device_id_type=MESH),
+        )
+
+    for ok, dev in greet:
+        signal(ok, dev)
+    close = len(greet)
 
     loads = [
         pltpu.make_async_copy(
@@ -72,30 +87,15 @@
     for c in loads:
         c.start()
 
-    barrier = pltpu.get_barrier_semaphore()
-    count = 0
-    greet = []
-    for dx in (-1, 0, 1):
-        for dy in (-1, 0, 1):
-            for side in (0, 1):
-                if dx == 0 and dy == 0 and side == 0:
-                    continue
-                ok = None if dy == 0 else (has_low if dy < 0 else has_high)
-                who = g if side == 0 else other
-                greet.append((ok, (who, lax.rem(gx + dx + GX, GX), gy + dy)))
     for y in range(GY):
         far = jnp.abs(gy - y) >= 2
-        greet.append((far, (1, gx, y)))
-        greet.append((both(far, g == 1), (0, gx, y)))
+        greet.append((far, (g, gx, y)))
+        greet.append((far, (other, gx, y)))
     for off in range(2, GX - 1):
-        greet.append((g == 1, (1, lax.rem(gx + off, GX), gy)))
-    for ok, dev in greet:
-        when(
-            ok,
-            lambda dev=dev: pl.semaphore_signal(
-                barrier, inc=1, device_id=dev, device_id_type=MESH
-            ),
-        )
+        greet.append((None, (g, lax.rem(gx + off, GX), gy)))
+    for ok, dev in greet[close:]:
+        signal(ok, dev)
+    for ok, _ in greet:
         count = count + (1 if ok is None else jnp.where(ok, 1, 0))
 
     for ok, row, urow, wrow in ((gy == 0, 0, 6, 7), (gy == GY - 1, LY + 2, 24, 24)):
@@ -109,7 +109,7 @@
 
         pl.when(ok)(clear)
 
-    for c in loads:
+    for c in loads[:3]:
         c.wait()
     wc[0, pl.ds(8, LY), :] = masks[0].astype(F32)
     wc[1, pl.ds(8, LY), :] = 0.1 - 0.15 * (0.25 * (1.0 + 3.0 * masks[1].astype(F32)))
@@ -137,8 +137,8 @@
                 )
         for dy, s, d in ((-1, 8, 24), (1, 22, 6)):
             halo(0, dy, ue.at[xs, pl.ds(s, 2), lanes], ue.at[xs, pl.ds(d, 2), lanes], who)
-        for dx, s, d in ((-1, 2, LX + 2), (1, LX, 0)):
-            halo(dx, 0, ue.at[pl.ds(s, 2), yu, lanes], ue.at[pl.ds(d, 2), yu, lanes], who)
+    for dx, s, d in ((-1, 2, LX + 2), (1, LX, 0)):
+        halo(dx, 0, ue.at[pl.ds(s, 2), yu, lanes], ue.at[pl.ds(d, 2), yu, lanes])
     for dy, s, d in ((-1, 8, 24), (1, 23, 7)):
         halo(0, dy, wc.at[:, pl.ds(s, 1)], wc.at[:, pl.ds(d, 1)])
     u_count = len(halos)
@@ -149,8 +149,16 @@
     for dx, sx, tx in ((-1, 2, LX + 2), (1, LX + 1, 1)):
         for dy, sy, ty in ((-1, 2, LY + 2), (1, LY + 1, 1)):
             halo(dx, dy, fi.at[sx, sy], fi.at[tx, ty])
-
-    for to, _, c in halos:
+    first_count = len(halos)
+    lanes2 = pl.ds(pl.multiple_of(other * HALF, HALF), HALF)
+    for dx, s, d in ((-1, 2, LX + 2), (1, LX, 0)):
+        halo(dx, 0, ue.at[pl.ds(s, 2), yu, lanes2], ue.at[pl.ds(d, 2), yu, lanes2])
+
+    for to, _, c in halos[:u_count]:
+        when(to, c.start)
+    for c in loads[3:]:
+        c.wait()
+    for to, _, c in halos[u_count:first_count]:
         when(to, c.start)
 
     def arrive(lo, hi):
@@ -193,86 +201,81 @@
         for y in rows:
             w[g, x, y] = row_step(v1, u1, x + 1, y + 1, x + 1, y + 8, y + 8)
 
-    def first_inner(x):
-        @pl.loop(0, 2)
-        def _(b):
-            first_rows(x, [2 + b * 7 + i for i in range(7)])
-
-    def second_inner(x):
-        @pl.loop(0, 2)
-        def _(b):
-            second_rows(x, [2 + b * 6 + i for i in range(6)])
-
     half = LX // 2
     inner = pl.ds(2, LY - 4)
     edges = (pl.ds(0, 2), pl.ds(LY - 2, 2))
 
-    def pieces(s):
-        near = [w.at[s, 2 + 2 * s + i, inner] for i in range(2)]
-        far = [w.at[s, 6 * s + i, inner] for i in range(2)]
-        rim = [w.at[s, pl.ds(half * s, half), e] for e in edges]
-        return near + far + rim
-
-    sends = [
-        remote(r, r, x_send.at[i], x_recv.at[i], partner) for i, r in enumerate(pieces(g))
-    ]
-    gets = [
-        remote(r, r, x_send.at[i], x_recv.at[i], partner)
-        for i, r in enumerate(pieces(other))
-    ]
-
-    arrive(0, u_count)
+    def plane_of(k, group):
+        near = jnp.where(k < 2, 2 + k, 3 - k)
+        x = jnp.where(k < 4, near, k)
+        return jnp.where(group == 0, x, LX - 1 - x)
+
+    def plane_ref(i, group):
+        return w.at[group, plane_of(i, group), inner]
+
+    def plane_send(i):
+        r = plane_ref(i, g)
+        return remote(r, r, x_send.at[i], x_recv.at[i], partner)
+
+    def rim_send(e, group):
+        r = w.at[group, pl.ds(half * group, half), edges[e]]
+        return remote(r, r, x_send.at[4 + e], x_recv.at[4 + e], partner)
+
+    arrive(0, 1)
+    for _, _, c in halos[first_count:]:
+        c.start()
 
     @pl.loop(0, LX + 2)
+    def _(k):
+        @pl.when(k == 1)
+        def _():
+            arrive(1, u_count)
+            arrive(first_count, len(halos))
+
+            @pl.loop(0, (LX + 2) // 2)
+            def _(x):
+                for i in range(2):
+                    u1[2 * x + i] = u_step(ue, 2 * x + i + 1)
+
+        @pl.when(k == 4)
+        def _():
+            arrive(u_count, u_count + 2)
+
+        x = jnp.where(k < 4, 2 + k, jnp.where(k < 6, 5 - k, k))
+        first_rows(jnp.where(g == 0, x, LX + 1 - x), range(2, LY))
+
+        @pl.when(k >= 2)
+        def _():
+            second_rows(plane_of(k - 2, g), range(2, LY - 2))
+
+        @pl.when(jnp.logical_and(k >= 2, k < 6))
+        def _():
+            plane_send(k - 2).start()
+
+    arrive(u_count + 2, first_count)
+
+    @pl.loop(0, (LX + 2) // 2)
     def _(x):
-        u1[x] = u_step(ue, x + 1)
-
-    @pl.loop(0, 4)
-    def _(i):
-        first_inner(2 + 2 * g + i)
-
-    for i in range(2):
-        second_inner(2 + 2 * g + i)
-        sends[i].start()
-
-    arrive(u_count, u_count + 2)
-    for i in range(2):
-        first_inner(8 * g + i)
-    for i in range(2):
-        second_inner(6 * g + i)
-        sends[2 + i].start()
-
-    @pl.loop(0, 4)
-    def _(i):
-        first_inner(6 * other + i)
-
-    arrive(u_count + 2, len(halos))
-
-    @pl.loop(0, LX + 2)
+        for i in range(2):
+            first_rows(2 * x + i, (0, 1, LY, LY + 1))
+
+    @pl.loop(0, half)
+    def _(h):
+        for i in range(2):
+            x = 2 * h + i
+            x = jnp.where(g == 0, x, LX - 1 - x)
+            second_rows(x, (0, 1, LY - 2, LY - 1))
+
+        @pl.when(h == 1)
+        def _():
+            for e in range(2):
+                rim_send(e, g).start()
+
+    @pl.loop(0, LX // 2)
     def _(x):
-        first_rows(x, (1, LY))
-
-    @pl.loop(1, LX + 1)
-    def _(x):
-        first_rows(x, (0, LY + 1))
-
-    for e in range(2):
-
-        @pl.loop(0, half)
-        def _(x, e=e):
-            second_rows(half * g + x, (0, 1) if e == 0 else (LY - 2, LY - 1))
-
-        sends[4 + e].start()
-
-    @pl.loop(0, half)
-    def _(x):
-        second_inner(half * other + x)
-        second_rows(half * other + x, (0, 1, LY - 2, LY - 1))
-
-    @pl.loop(0, LX)
-    def _(x):
-        c = u_step(u1, x + 1)[8:24]
-        base_out[x] = jnp.where(g == 0, c[:, :HALF], c[:, HALF:])
+        for i in range(2):
+            c = u_step(u1, 2 * x + i + 1)[8:24]
+            base_out[2 * x + i] = jnp.where(g == 0, c[:, :HALF], c[:, HALF:])
 
     def gram_rows(a, b, x, lo, n, acc, unroll):
         def step(y, acc):
@@ -289,65 +292,76 @@
         part = jnp.where(col == 8 + 8 * g + j, jnp.sum(own[j], axis=1, keepdims=True), part)
     cross = zeros
     for i in range(4):
-        gets[i].wait_recv()
-        x = (2 + 2 * other if i < 2 else 6 * other) + i % 2
-        cross = gram_rows(1, 0, x, 2, LY - 4, cross, 4)
+        plane_send(i).wait_recv()
+        cross = gram_rows(1, 0, plane_of(i, other), 2, LY - 4, cross, 4)
     for e in range(2):
-        gets[4 + e].wait_recv()
-        cross = lax.fori_loop(
-            0, half,
-            lambda x, acc: gram_rows(1, 0, half * other + x, e * (LY - 2), 2, acc, 2),
-            cross,
-        )
+        rim_send(e, other).wait_recv()
+
+    def rim_gram(x, acc):
+        acc = gram_rows(1, 0, half * other + x, 0, 2, acc, 2)
+        return gram_rows(1, 0, half * other + x, LY - 2, 2, acc, 2)
+
+    cross = lax.fori_loop(0, half, rim_gram, cross)
     for j in range(NF):
         part = jnp.where(col == j, jnp.sum(cross[j], axis=1, keepdims=True), part)
     me = g * GY + gy
+    sub8 = lax.broadcasted_iota(jnp.int32, (NF, 128), 0)
+    quarter = sub8 & 3
+    wide = jnp.where(quarter == 0, part, 0.0)
+    for k in range(1, 4):
+        wide = jnp.where(quarter == k, pltpu.roll(part, 32 * k, 1), wide)
+    part = jnp.concatenate(
+        [jnp.sum(wide[4 * r : 4 * r + 4], axis=0, keepdims=True) for r in range(2)], axis=0
+    )
     tile[0] = part
     al[me] = part
 
-    def p_copy(off):
-        dev = (1, gx, lax.rem(gy + off, GY))
-        return remote(tile.at[0], al.at[me], p_send.at[off], p_recv.at[me], dev)
-
-    for off in P_ORDER:
-        when(g == 0 if off == 0 else None, p_copy(off).start)
-
-    tail_ref = w.at[0, pl.ds(half, half)]
-    tail = remote(tail_ref, tail_ref, x_send.at[6], x_recv.at[6], (1, gx, gy))
-    final = remote(gs, gs, x_send.at[7], x_recv.at[7], (0, gx, gy))
-
-    @pl.when(g == 0)
-    def _():
-        tail.start()
-        final.wait_recv()
+    def p_copy(i):
+        off, swap = P_ORDER[i]
+        dev = (other if swap else g, gx, lax.rem(gy + off, GY))
+        return remote(tile.at[0], al.at[me], p_send.at[i], p_recv.at[me], dev)
+
+    for i in range(len(P_ORDER)):
+        p_copy(i).start()
+
+    def tail(i):
+        lo, n = TAIL[i]
+        r = w.at[0, pl.ds(lo, n)]
+        return remote(r, r, x_send.at[6 + i], x_recv.at[6 + i], (1, gx, gy))
+
+    def tail_start(i):
+        @pl.when(g == 0)
+        def _():
+            tail(i).start()
 
     def z_copy(off):
-        dev = (1, lax.rem(gx + off, GX), gy)
+        dev = (g, lax.rem(gx + off, GX), gy)
         return remote(tile.at[1], zl.at[gx], z_send.at[off], z_recv.at[gx], dev)
 
-    @pl.when(g == 1)
-    def _():
-        for s in range(2 * GY):
-            c = remote(tile.at[0], al.at[s], p_send.at[0], p_recv.at[s], partner)
-            when(None if s < GY else gy != s - GY, c.wait_recv)
-        total = al[0]
-        for s in range(1, 2 * GY):
-            total = total + al[s]
-        tile[1] = total
-        zl[gx] = total
-        for off in Z_ORDER:
-            z_copy(off).start()
-        for s in range(GX):
-            c = remote(tile.at[1], zl.at[s], z_send.at[0], z_recv.at[s], partner)
-            when(gx != s, c.wait_recv)
-        total = zl[0]
-        for s in range(1, GX):
-            total = total + zl[s]
-        gs[...] = total * (1.0 / CELLS)
-        final.start()
-
-    gram = gs[...]
-    sub8 = lax.broadcasted_iota(jnp.int32, (NF, 128), 0)
+    tail_start(0)
+    for s in range(2 * GY):
+        c = remote(tile.at[0], al.at[s], p_send.at[0], p_recv.at[s], partner)
+        when(me != s, c.wait_recv)
+    total = al[0]
+    for s in range(1, 2 * GY):
+        total = total + al[s]
+    tile[1] = total
+    zl[gx] = total
+    for off in Z_ORDER:
+        z_copy(off).start()
+    tail_start(1)
+    for s in range(GX):
+        c = remote(tile.at[1], zl.at[s], z_send.at[0], z_recv.at[s], partner)
+        when(gx != s, c.wait_recv)
+    total = zl[0]
+    for s in range(1, GX):
+        total = total + zl[s]
+
+    total = total * (1.0 / CELLS)
+    wide = jnp.where(sub8 < 4, total[0:1], total[1:2])
+    gram = wide
+    for k in range(1, 4):
+        gram = jnp.where(quarter == k, pltpu.roll(wide, 128 - 32 * k, 1), gram)
     g01 = jnp.zeros((NF, 128), F32)
     for j in range(NF):
         row = jnp.where(col == sub8, gram[j : j + 1, :], 0.0)
@@ -373,24 +387,24 @@
 
     @pl.when(g == 1)
     def _():
-        tail.wait_recv()
+        for i in range(2):
+            tail(i).wait_recv()
 
     for to, _, c in halos:
         when(to, c.wait_send)
-    for c in sends:
-        c.wait_send()
-    for off in P_ORDER:
-        when(g == 0 if off == 0 else None, p_copy(off).wait_send)
+    for i in range(4):
+        plane_send(i).wait_send()
+    for e in range(2):
+        rim_send(e, g).wait_send()
+    for i in range(len(P_ORDER)):
+        p_copy(i).wait_send()
+    for off in Z_ORDER:
+        z_copy(off).wait_send()
 
     @pl.when(g == 0)
     def _():
-        tail.wait_send()
-
-    @pl.when(g == 1)
-    def _():
-        final.wait_send()
-        for off in Z_ORDER:
-            z_copy(off).wait_send()
+        for i in range(2):
+            tail(i).wait_send()
 
 
 def apply_kernel(
@@ -398,12 +412,12 @@
 ):
     g = lax.axis_index("grp")
     small = [
-        pltpu.make_async_copy(base, base_hbm, out_sem.at[4 * NF]),
-        pltpu.make_async_copy(growth, growth_hbm, out_sem.at[4 * NF + 1]),
+        pltpu.make_async_copy(base, base_hbm, out_sem.at[PARTS * NF]),
+        pltpu.make_async_copy(growth, growth_hbm, out_sem.at[PARTS * NF + 1]),
     ]
     for c in small:
         c.start()
-    step = LX // 4
+    step = LX // PARTS
 
     def out_copy(q, f):
         r = pl.ds(q * step, step)
@@ -428,7 +442,7 @@
 
             return lax.fori_loop(0, LY, row, carry, unroll=4)
 
-        for q in range(4):
+        for q in range(PARTS):
             lax.fori_loop(q * step, (q + 1) * step, plane, 0)
             for f in range(NF):
                 out_copy(q, f).start()
@@ -441,7 +455,7 @@
     def _():
         emit(2)
 
-    for q in range(4):
+    for q in range(PARTS):
         for f in range(NF):
             out_copy(q, f).wait()
     for c in small:
@@ -470,16 +484,15 @@
             pltpu.VMEM((LX + 2, 32, NZ), F32),
             pltpu.VMEM((2, LY, NZ), jnp.int32),
             pltpu.VMEM((2, 32, NZ), F32),
-            pltpu.VMEM((2, NF, 128), F32),
-            pltpu.VMEM((2 * GY, NF, 128), F32),
-            pltpu.VMEM((GX, NF, 128), F32),
-            pltpu.VMEM((NF, 128), F32),
+            pltpu.VMEM((2, 2, 128), F32),
+            pltpu.VMEM((2 * GY, 2, 128), F32),
+            pltpu.VMEM((GX, 2, 128), F32),
             dma((NF + 3,)),
             dma((32,)),
             dma((32,)),
             dma((8,)),
             dma((8,)),
-            dma((GY,)),
+            dma((2 * GY,)),
             dma((2 * GY,)),
             dma((GX,)),
             dma((GX,)),
@@ -497,7 +510,7 @@
         ],
         in_specs=[vmem] * 4,
         out_specs=[hbm] * 3,
-        scratch_shapes=[pltpu.VMEM((LX, LY, NF, NZ), F32), dma((4 * NF + 2,))],
+        scratch_shapes=[pltpu.VMEM((LX, LY, NF, NZ), F32), dma((PARTS * NF + 2,))],
         compiler_params=pltpu.CompilerParams(vmem_limit_bytes=16 << 20),
     )(stepped, base, coef, growth)
     return base, ortho, growth.reshape(2 * NF)

time: 50.4 us -> 47.6 us (0.944)
  Pallas kernels: 49.3 us -> 46.5 us
    pallas_call x1, Pallas kernels: 47.3 us -> 44.6 us  [body(): pl.pallas_call(kernel, out_shape=[pltpu.VMEM((2, LX, LY, NF, NZ), F32), p...]
where the time goes in v3:
time: 47.6 us; the launch traced here: 47.2 us
  Pallas kernels  46.5 us (98%)
  between operations  0.64 us (1%)
    pallas_call x1, Pallas kernels, body(): pl.pallas_call(kernel, out_shape=[pltpu.VMEM((2, LX, LY, NF, NZ), F32), p...  44.6 us
    pallas_call x1, Pallas kernels, body(): pl.pallas_call(apply_kernel, out_shape=[jax.ShapeDtypeStruct(base_flow.sh...  1.88 us

profile of v3, /device:TPU:1, one launch (start us, length us, event | category | flops | bytes accessed | tf_op | source)
XLA Modules:
  0.0 47.2 jit_solution(6554956556875652378)
XLA Ops:
  0.6 44.6 %shard_map.67 = (f32[2,8,16,8,256]{4,3,2,1,0:T(8,128)S(1)}, f32[8,16,128]{2,1,0:T(8,128)S(1)}, f32[8,128]{1,0:T(8,128)S(1)}, f32[1,16]{1,0:T(1,128)S(1)}) custom-call(f32[8,16,128]{2,1,0:T(8,128)} %base_hbm.1, f32[8,8,16,256]{3,2,1,0:T(8,128)} %fields_hbm.1, s32[16,256]{1,0:T(8,128)} %wall_hbm.1, s32[16,256]{1,0:T(8,128)} %cond_hbm.1), custom_call_target="tpu_custom_call" | custom-call | tf_op jit(solution)/shard_map/pallas_call | solution.py:470
  45.3 1.9 %shard_map.68 = (f32[8,16,128]{2,1,0:T(8,128)}, f32[8,8,16,256]{3,2,1,0:T(8,128)}, f32[1,16]{1,0:T(1,128)}) custom-call(f32[2,8,16,8,256]{4,3,2,1,0:T(8,128)S(1)} %get-tuple-element.10.w, f32[8,16,128]{2,1,0:T(8,128)S(1)} %get-tuple-element.11.base, f32[8,128]{1,0:T(8,128)S(1)} %get-tuple-element.12.coef, f32[1,16]{1,0:T(1,128)S(1)} %get-tuple-element.13.growth), custom_call_target="tpu_custom_call" | custom-call | tf_op jit(solution)/shard_map/pallas_call | solution.py:504

commit v4 on v3

--- a/solution.py
+++ b/solution.py
@@ -13,7 +13,7 @@
 PARTS = 2
 CELLS = 4194304.0
 P_ORDER = tuple((off, swap) for off in (4, 3, 5, 2, 6, 1, 7, 0) for swap in (1, 0) if off or swap)
-TAIL = ((4, 2), (6, 2))
+TAIL = ((4, 1), (5, 2), (7, 1))
 Z_ORDER = (8, 7, 9, 6, 10, 5, 11, 4, 12, 3, 13, 2, 14, 1, 15)
 
 
@@ -271,6 +271,18 @@
             for e in range(2):
                 rim_send(e, g).start()
 
+    def tail(i):
+        lo, n = TAIL[i]
+        r = w.at[0, pl.ds(lo, n)]
+        return remote(r, r, x_send.at[6 + i], x_recv.at[6 + i], (1, gx, gy))
+
+    def tail_start(i):
+        @pl.when(g == 0)
+        def _():
+            tail(i).start()
+
+    tail_start(0)
+
     @pl.loop(0, LX // 2)
     def _(x):
         for i in range(2):
@@ -324,21 +336,11 @@
     for i in range(len(P_ORDER)):
         p_copy(i).start()
 
-    def tail(i):
-        lo, n = TAIL[i]
-        r = w.at[0, pl.ds(lo, n)]
-        return remote(r, r, x_send.at[6 + i], x_recv.at[6 + i], (1, gx, gy))
-
-    def tail_start(i):
-        @pl.when(g == 0)
-        def _():
-            tail(i).start()
-
     def z_copy(off):
         dev = (g, lax.rem(gx + off, GX), gy)
         return remote(tile.at[1], zl.at[gx], z_send.at[off], z_recv.at[gx], dev)
 
-    tail_start(0)
+    tail_start(1)
     for s in range(2 * GY):
         c = remote(tile.at[0], al.at[s], p_send.at[0], p_recv.at[s], partner)
         when(me != s, c.wait_recv)
@@ -349,7 +351,7 @@
     zl[gx] = total
     for off in Z_ORDER:
         z_copy(off).start()
-    tail_start(1)
+    tail_start(2)
     for s in range(GX):
         c = remote(tile.at[1], zl.at[s], z_send.at[0], z_recv.at[s], partner)
         when(gx != s, c.wait_recv)
@@ -374,10 +376,12 @@
     m = jnp.concatenate([top, low], axis=0)
     sub = lax.broadcasted_iota(jnp.int32, (2 * NF, 128), 0)
     col16 = lax.broadcasted_iota(jnp.int32, (2 * NF, 128), 1)
+    spread = [jnp.broadcast_to(m[:, j : j + 1], m.shape) for j in range(2 * NF)]
     for k in range(2 * NF - 1):
-        pivot = m[k : k + 1, :]
-        factor = m[:, k : k + 1] / pivot[:, k : k + 1]
-        m = m - jnp.where(sub > k, factor, 0.0) * pivot
+        factor = jnp.where(sub > k, spread[k] / spread[k][k : k + 1, :], 0.0)
+        for j in range(k + 1, 2 * NF):
+            spread[j] = spread[j] - factor * spread[j][k : k + 1, :]
+        m = m - factor * m[k : k + 1, :]
     diag = jnp.where(col16 == sub, m, 0.0)
     root_row = jnp.sqrt(jnp.sum(diag, axis=0, keepdims=True))
     root_col = jnp.sqrt(jnp.sum(diag, axis=1, keepdims=True))
@@ -387,7 +391,7 @@
 
     @pl.when(g == 1)
     def _():
-        for i in range(2):
+        for i in range(len(TAIL)):
             tail(i).wait_recv()
 
     for to, _, c in halos:
@@ -403,7 +407,7 @@
 
     @pl.when(g == 0)
     def _():
-        for i in range(2):
+        for i in range(len(TAIL)):
             tail(i).wait_send()
 
 
@@ -440,7 +444,7 @@
                 o[x, y] = acc
                 return carry
 
-            return lax.fori_loop(0, LY, row, carry, unroll=4)
+            return lax.fori_loop(0, LY, row, carry, unroll=8)
 
         for q in range(PARTS):
             lax.fori_loop(q * step, (q + 1) * step, plane, 0)
@@ -490,8 +494,8 @@
             dma((NF + 3,)),
             dma((32,)),
             dma((32,)),
-            dma((8,)),
-            dma((8,)),
+            dma((9,)),
+            dma((9,)),
             dma((2 * GY,)),
             dma((2 * GY,)),
             dma((GX,)),

time: 47.6 us -> 46.4 us (0.975)
  Pallas kernels: 46.5 us -> 45.6 us
    pallas_call x1, Pallas kernels: 44.6 us -> 43.9 us  [body(): pl.pallas_call(kernel, out_shape=[pltpu.VMEM((2, LX, LY, NF, NZ), F32), p...]
where the time goes in v4:
time: 46.4 us; the launch traced here: 46.3 us
  Pallas kernels  45.6 us (98%)
  between operations  0.64 us (1%)
    pallas_call x1, Pallas kernels, body(): pl.pallas_call(kernel, out_shape=[pltpu.VMEM((2, LX, LY, NF, NZ), F32), p...  43.9 us
    pallas_call x1, Pallas kernels, body(): pl.pallas_call(apply_kernel, out_shape=[jax.ShapeDtypeStruct(base_flow.sh...  1.74 us

profile of v4, /device:TPU:1, one launch (start us, length us, event | category | flops | bytes accessed | tf_op | source)
XLA Modules:
  0.0 46.3 jit_solution(11986567605465969797)
XLA Ops:
  0.6 43.9 %shard_map.67 = (f32[2,8,16,8,256]{4,3,2,1,0:T(8,128)S(1)}, f32[8,16,128]{2,1,0:T(8,128)S(1)}, f32[8,128]{1,0:T(8,128)S(1)}, f32[1,16]{1,0:T(1,128)S(1)}) custom-call(f32[8,16,128]{2,1,0:T(8,128)} %base_hbm.1, f32[8,8,16,256]{3,2,1,0:T(8,128)} %fields_hbm.1, s32[16,256]{1,0:T(8,128)} %wall_hbm.1, s32[16,256]{1,0:T(8,128)} %cond_hbm.1), custom_call_target="tpu_custom_call" | custom-call | tf_op jit(solution)/shard_map/pallas_call | solution.py:474
  44.5 1.7 %shard_map.68 = (f32[8,16,128]{2,1,0:T(8,128)}, f32[8,8,16,256]{3,2,1,0:T(8,128)}, f32[1,16]{1,0:T(1,128)}) custom-call(f32[2,8,16,8,256]{4,3,2,1,0:T(8,128)S(1)} %get-tuple-element.10.w, f32[8,16,128]{2,1,0:T(8,128)S(1)} %get-tuple-element.11.base, f32[8,128]{1,0:T(8,128)S(1)} %get-tuple-element.12.coef, f32[1,16]{1,0:T(1,128)S(1)} %get-tuple-element.13.growth), custom_call_target="tpu_custom_call" | custom-call | tf_op jit(solution)/shard_map/pallas_call | solution.py:508

commit v5 on v4

--- a/solution.py
+++ b/solution.py
@@ -352,6 +352,14 @@
     for off in Z_ORDER:
         z_copy(off).start()
     tail_start(2)
+    for to, _, c in halos:
+        when(to, c.wait_send)
+    for i in range(4):
+        plane_send(i).wait_send()
+    for e in range(2):
+        rim_send(e, g).wait_send()
+    for i in range(len(P_ORDER)):
+        p_copy(i).wait_send()
     for s in range(GX):
         c = remote(tile.at[1], zl.at[s], z_send.at[0], z_recv.at[s], partner)
         when(gx != s, c.wait_recv)
@@ -394,14 +402,6 @@
         for i in range(len(TAIL)):
             tail(i).wait_recv()
 
-    for to, _, c in halos:
-        when(to, c.wait_send)
-    for i in range(4):
-        plane_send(i).wait_send()
-    for e in range(2):
-        rim_send(e, g).wait_send()
-    for i in range(len(P_ORDER)):
-        p_copy(i).wait_send()
     for off in Z_ORDER:
         z_copy(off).wait_send()
 

time: 46.4 us -> 46.3 us (level)
  no operation moved by 1% of the time
where the time goes in v5:
time: 46.3 us; the launch traced here: 46.2 us
  Pallas kernels  45.6 us (98%)
  between operations  0.64 us (1%)
    pallas_call x1, Pallas kernels, body(): pl.pallas_call(kernel, out_shape=[pltpu.VMEM((2, LX, LY, NF, NZ), F32), p...  43.8 us
    pallas_call x1, Pallas kernels, body(): pl.pallas_call(apply_kernel, out_shape=[jax.ShapeDtypeStruct(base_flow.sh...  1.74 us

profile of v5, /device:TPU:1, one launch (start us, length us, event | category | flops | bytes accessed | tf_op | source)
XLA Modules:
  0.0 46.2 jit_solution(3738736983593853659)
XLA Ops:
  0.6 43.8 %shard_map.67 = (f32[2,8,16,8,256]{4,3,2,1,0:T(8,128)S(1)}, f32[8,16,128]{2,1,0:T(8,128)S(1)}, f32[8,128]{1,0:T(8,128)S(1)}, f32[1,16]{1,0:T(1,128)S(1)}) custom-call(f32[8,16,128]{2,1,0:T(8,128)} %base_hbm.1, f32[8,8,16,256]{3,2,1,0:T(8,128)} %fields_hbm.1, s32[16,256]{1,0:T(8,128)} %wall_hbm.1, s32[16,256]{1,0:T(8,128)} %cond_hbm.1), custom_call_target="tpu_custom_call" | custom-call | tf_op jit(solution)/shard_map/pallas_call | solution.py:474
  44.4 1.7 %shard_map.68 = (f32[8,16,128]{2,1,0:T(8,128)}, f32[8,8,16,256]{3,2,1,0:T(8,128)}, f32[1,16]{1,0:T(1,128)}) custom-call(f32[2,8,16,8,256]{4,3,2,1,0:T(8,128)S(1)} %get-tuple-element.10.w, f32[8,16,128]{2,1,0:T(8,128)S(1)} %get-tuple-element.11.base, f32[8,128]{1,0:T(8,128)S(1)} %get-tuple-element.12.coef, f32[1,16]{1,0:T(1,128)S(1)} %get-tuple-element.13.growth), custom_call_target="tpu_custom_call" | custom-call | tf_op jit(solution)/shard_map/pallas_call | solution.py:508
